TPU v7x, 32 devices: a whole 2x2x4 slice. The times are simulated.
32 devices in a mesh: dp: 8 (over z, x), row: 2 (over y), col: 2 (over core).
Axes of the slice: x: 2, y: 2, z: 4, core: 2. Of those that a mesh axis runs over, the one named last changes fastest.
Arguments:
- latents: bfloat16 [4096, 768], P(('dp', 'row'), 'col'), may hold values from -6 to 6
- labels: int32 [16], P('dp'), may hold values from 0 to 999
- timesteps: int32 [16], P('dp'), may hold values from 0 to 999
- class_table: bfloat16 [1000, 768], P(None, 'row'), may hold values from -6 to 6
- mod_weight: bfloat16 [768, 6, 768], P('row', None, 'col'), may hold values from -0.21875 to 0.21875
- mod_bias: bfloat16 [6, 768], P(None, 'col'), may hold values from -3 to 3
- qkv_weight: bfloat16 [768, 12, 3, 64], P('col', 'row'), may hold values from -0.21875 to 0.21875
- query_value_bias: bfloat16 [2, 12, 64], P(None, ('row', 'col')), may hold values from -3 to 3
- out_weight: bfloat16 [12, 64, 768], P('row', None, 'col'), may hold values from -0.21875 to 0.21875
- out_bias: bfloat16 [768], P('col'), may hold values from -3 to 3
- up_weight: bfloat16 [768, 3072], P('col', 'row'), may hold values from -0.21875 to 0.21875
- up_bias: bfloat16 [3072], P('row'), may hold values from -3 to 3
- down_weight: bfloat16 [3072, 768], P('row', 'col'), may hold values from -0.109375 to 0.109375
- down_bias: bfloat16 [768], P('col'), may hold values from -3 to 3
- cotangent: bfloat16 [4096, 768], P(('dp', 'row'), 'col'), may hold values from -6 to 6
Outputs:
- output: bfloat16 [4096, 768], P(('dp', 'row'), 'col')
- grad_latents: float32 [4096, 768], P(('dp', 'row'), 'col')
- grad_cond: float32 [16, 768], P('dp', 'row')
- grad_mod_weight: float32 [768, 6, 2, 384], P('row', None, 'col', 'dp')
- grad_mod_bias: float32 [6, 2, 384], P(None, 'col', 'dp')
- grad_qkv_weight: float32 [2, 384, 12, 3, 64], P('col', 'dp', 'row')
- grad_query_value_bias: float32 [2, 12, 64], P(None, ('row', 'col'), 'dp')
- grad_out_weight: float32 [12, 64, 2, 384], P('row', None, 'col', 'dp')
- grad_out_bias: float32 [2, 384], P('col', 'dp')
- grad_up_weight: float32 [768, 2, 1536], P('col', 'row', 'dp')
- grad_up_bias: float32 [2, 1536], P('row', 'dp')
- grad_down_weight: float32 [3072, 2, 384], P('row', 'col', 'dp')
- grad_down_bias: float32 [2, 384], P('col', 'dp')
All inputs are finite; a program needn't handle non-finite values.
Results may differ from a plain program's by a relative error of at most 0.017.
Values may be sent and summed in bfloat16 or wider, within the bound.
No kernel may reach another device: no remote copies, remote signals or barrier semaphores. Data moves between devices by JAX's collectives and lax.ppermute only.
A program may use at most 128 MiB of HBM per device.

v0:
```python
import functools
import math

import jax
import jax.numpy as jnp
from jax import lax
from jax.experimental import pallas as pl
from jax.experimental.pallas import tpu as pltpu
from jax.sharding import PartitionSpec as P

D = 768
HALF = 384
SEQ = 256
HEADS = 6
HD = 64
QKV = HEADS * 3 * HD
FEED = 1536
EPSILON = 1e-06
HIGH = lax.Precision.HIGHEST
F32 = jnp.float32
BF16 = jnp.bfloat16
SWAP = [(0, 1), (1, 0)]
ALPHA = 0.7978845608
CUBIC = 0.044715


def mm(first, second, dims, precision=None):
    return lax.dot_general(
        first, second, ((dims[:1], dims[1:]), ((), ())), precision=precision, preferred_element_type=F32
    )


def call(kernel, outs, inputs, micros, name, after=(), scratch=(), limit=16):
    count = len(after)

    def body(*refs):
        kernel(*refs[count:])

    return pl.pallas_call(
        body if count else kernel,
        out_shape=[jax.ShapeDtypeStruct(s, t) for s, t in outs],
        in_specs=[pl.BlockSpec(memory_space=pl.ANY)] * count
        + [pl.BlockSpec(memory_space=pltpu.VMEM)] * len(inputs),
        out_specs=[pl.BlockSpec(memory_space=pltpu.VMEM)] * len(outs),
        scratch_shapes=list(scratch),
        compiler_params=pltpu.CompilerParams(vmem_limit_bytes=limit * 1024 * 1024),
        cost_estimate=pl.CostEstimate(flops=int(micros * 1.15e9), bytes_accessed=1024, transcendentals=0),
        name=name,
    )(*after, *inputs)


def row_mean(values):
    return jnp.sum(values, axis=1, keepdims=True) * (1.0 / D)


def norm_of(values):
    centred = values - row_mean(values)
    inverse = lax.rsqrt(row_mean(centred * centred) + EPSILON)
    return centred * inverse, inverse


def halves(first, second):
    return jnp.concatenate([first, second], axis=1)


def blocks(step=64):
    return [slice(i, i + step) for i in range(0, SEQ, step)]


def mod_kernel(looked, cosine, sine, weight, part, soft, cond):
    place = lax.broadcasted_iota(jnp.int32, (16, HALF), 0)
    both = looked[...] + jnp.where(lax.axis_index("row") == 0, cosine[...], sine[...])
    cond[...] = both
    values = jnp.where(place == 0, both[0:1, :], jnp.where(place == 1, both[1:2, :], 0.0))
    soft16 = (values / (1.0 + jnp.exp(-values))).astype(BF16)
    soft[...] = soft16.astype(F32)[0:2]
    part[...] = jnp.zeros((16, HALF), F32)
    for k in range(6):
        pair = mm(soft16, weight[k], (1, 0))
        part[k : k + 1, :] = pair[0:1]
        part[8 + k : 9 + k, :] = pair[1:2]


def mix_kernel(part, part_recv, bias, out_bias, down_bias, pair_bias, keep, other):
    total = part[...] + part_recv[...]
    here = lax.axis_index("col") == 0
    shift = bias[...].astype(F32)
    keep[...] = jnp.where(here, total[0:6], total[8:14]) + shift
    other[0:6, :] = jnp.where(here, total[8:14], total[0:6]) + shift
    other[6:8, :] = jnp.zeros((2, HALF), F32)
    other[8:16, :] = jnp.zeros((8, HALF), F32)
    other[8:9, :] = out_bias[...].astype(F32).reshape(1, HALF)
    other[9:10, :] = down_bias[...].astype(F32).reshape(1, HALF)
    for i in range(2):
        for h in range(HEADS // 2):
            spot = (3 * i + h) * HD
            other[10:11, spot : spot + HD] = pair_bias[i, h : h + 1, :].astype(F32)


def pack_kernel(first, second, out):
    out[0:SEQ, :] = first[...]
    out[SEQ : 2 * SEQ, :] = second[...]


def pick_image(own, col, change, rows):
    same = lax.axis_index("row") == lax.axis_index("col")
    later = slice(rows.start + SEQ, rows.stop + SEQ)
    left = jnp.where(same, own[rows, :].astype(F32), change[later, :].astype(F32))
    right = jnp.where(same, col[rows, :].astype(F32), change[rows, :].astype(F32))
    return halves(left, right)


def norm_kernel(own, col, change, lat, normal):
    for rows in blocks():
        values = pick_image(own, col, change, rows)
        lat[rows, :] = values.astype(BF16)
        normal[rows, :] = norm_of(values)[0]


def first_kernel(
    normal, keep, other, other_col, qkv_own, qkv_peer, out_own, out_peer,
    mod, bias, normed_own, normed_peer, packed, attended, part,
):
    mods = halves(keep[...], other_col[0:6, :])
    mod[...] = mods
    shift, scale = mods[0:1], 1.0 + mods[1:2]
    for rows in blocks():
        normed = (normal[rows, :] * scale + shift).astype(BF16)
        normed_own[rows, :] = normed[:, :HALF]
        normed_peer[rows, :] = normed[:, HALF:]
    bias[...] = halves(other[8:16, :], other_col[8:16, :])
    place = lax.broadcasted_iota(jnp.int32, (16, SEQ), 0)
    one_hot = (place == 0).astype(BF16)
    mine = lax.axis_index("col")
    front = jnp.where(mine == 0, other[10:11, :], other_col[10:11, :])
    back = jnp.where(mine == 0, other_col[10:11, :], other[10:11, :])
    wide = lax.broadcasted_iota(jnp.int32, (16, 3 * HD), 0)
    for h in range(HEADS):
        rows = slice(h * 192, h * 192 + 192)
        source, spot = (front if h < 3 else back), (h % 3) * HD
        line = jnp.concatenate(
            [source[:, spot : spot + HD], jnp.zeros((1, HD), F32), source[:, 192 + spot : 192 + spot + HD]], axis=1
        )
        full = mm(qkv_own[rows, :], normed_own[...], (1, 1))
        full = full + mm(qkv_peer[rows, :], normed_peer[...], (1, 1))
        full = full + mm(jnp.where(wide == 0, line, 0.0).astype(BF16), one_hot, (0, 0))
        full = full.astype(BF16)
        packed[rows, :] = full
        query, key, value = full[0:64], full[64:128], full[128:192]
        scores = mm(key, query, (0, 0)) * 0.125
        expon = jnp.exp(scores - jnp.max(scores, axis=0, keepdims=True))
        probs = (expon * (1.0 / jnp.sum(expon, axis=0, keepdims=True))).astype(BF16)
        attended[h * 64 : h * 64 + 64, :] = mm(value, probs, (1, 0)).astype(BF16)
    part[:, :HALF] = mm(attended[...], out_own[...], (0, 0)).astype(BF16)
    part[:, HALF:] = mm(attended[...], out_peer[...], (0, 0)).astype(BF16)


def early_kernel(own, col, change, mod, down_own, down_peer, cot, grad_own, grad_peer, grad_active):
    gate = mod[5:6, :]
    for rows in blocks():
        values = pick_image(own, col, change, rows)
        cot[rows, :] = values.astype(BF16)
        grads = (values * gate).astype(BF16)
        grad_own[rows, :] = grads[:, :HALF]
        grad_peer[rows, :] = grads[:, HALF:]
    for cols in [slice(j, j + 256) for j in range(0, FEED, 256)]:
        grad_active[:, cols] = mm(grad_own[...], down_own[cols, :], (1, 1)) + mm(
            grad_peer[...], down_peer[cols, :], (1, 1)
        )


def branch(part, part_recv, bias, rows):
    return part[rows, :].astype(F32) + part_recv[rows, :].astype(F32) + bias


def resid_of(lat, mod, bias, part, part_recv, rows):
    gate = mod[2:3, :]
    one = branch(part, part_recv, bias[0:1, :], rows)
    return lat[rows, :].astype(F32) + gate * one, one


def second_kernel(
    lat, mod, bias, part, part_recv, up_own, up_peer, up_bias, grad_active,
    normed_own, active, hidden, part_two,
):
    shift, scale = mod[3:4, :], 1.0 + mod[4:5, :]
    for rows in blocks():
        resid, unused = resid_of(lat, mod, bias, part, part_recv, rows)
        normal, unused = norm_of(resid)
        normed = (normal * scale + shift).astype(BF16)
        normed_own[rows, :] = normed[:, :HALF]
        hidden[rows, FEED:] = normed[:, HALF:]
    shift_up = up_bias[...].astype(F32).reshape(1, FEED)
    for cols in [slice(j, j + 256) for j in range(0, FEED, 256)]:
        pre = mm(normed_own[...], up_own[:, cols], (1, 0)) + mm(hidden[:, FEED:], up_peer[:, cols], (1, 0))
        pre = pre + shift_up[:, cols]
        square = pre * pre
        bend = jnp.tanh(ALPHA * (pre + CUBIC * (pre * square)))
        half = 0.5 * (1.0 + bend)
        active[:, cols] = (pre * half).astype(BF16)
        slope = half + 0.5 * pre * (1.0 - bend * bend) * (ALPHA * (1.0 + (3.0 * CUBIC) * square))
        hidden[:, cols] = (grad_active[:, cols] * slope).astype(BF16)
    part_two[:, :HALF] = mm(hidden[:, :FEED], up_own[...], (1, 1)).astype(BF16)
    part_two[:, HALF:] = mm(hidden[:, :FEED], up_peer[...], (1, 1)).astype(BF16)


def down_kernel(active, cot, down_own, down_peer, part, sums):
    sums[...] = jnp.zeros((8, D), F32)
    for cols, weight in ((slice(0, HALF), down_own), (slice(HALF, D), down_peer)):
        here = mm(active[...], weight[...], (1, 0)).astype(BF16)
        part[:, cols] = here
        sums[0:1, cols] = jnp.sum(here.astype(F32) * cot[:, cols].astype(F32), axis=0, keepdims=True)


def spots(left, bit):
    step = 1 << (len(left) - 1 - left.index(bit))
    return step, [q for q in range(1 << len(left)) if q & step == 0]


def bit_here(bit):
    return lax.rem(lax.div(lax.axis_index("dp"), 1 << bit), 2)


def split_store(full, left, bit, send, keep):
    here = bit_here(bit)
    size = full.shape[0] >> len(left)
    step, places = spots(left, bit)
    for q, place in enumerate(places):
        low = full[place * size : (place + 1) * size]
        high = full[(place + step) * size : (place + step + 1) * size]
        keep[q] = jnp.where(here == 0, low, high).astype(BF16)
        send[q] = jnp.where(here == 0, high, low).astype(BF16)


def tokens(own, recv, axis=0):
    return jnp.concatenate([own[...], recv[...]], axis=axis)


def up_grad_kernel(left, bit, normed, hidden, hidden_recv, send, keep, bias):
    rows = jnp.concatenate([normed[...], hidden_recv[:, FEED:]], axis=0)
    grads = jnp.concatenate([hidden[:, :FEED], hidden_recv[:, :FEED]], axis=0)
    ones = jnp.ones((16, 2 * SEQ), BF16)
    bias[...] = mm(ones, grads, (1, 0))[0:1]
    split_store(mm(grads, rows, (0, 0)), left, bit, send, keep)


def down_grad_kernel(left, bit, grad, grad_recv, active, active_recv, send, keep, bias):
    grads = tokens(grad, grad_recv)
    acts = tokens(active, active_recv)
    ones = jnp.ones((16, 2 * SEQ), BF16)
    bias[...] = mm(ones, grads, (1, 0))[0:1]
    split_store(mm(grads, acts, (0, 0)), left, bit, send, keep)


def third_kernel(
    lat, mod, bias, part, part_recv, grad_two, grad_two_recv, cot, packed, sums,
    qkv_own, qkv_peer, out_own, out_peer,
    grad_resid, grad_own, grad_packed, part_three, grad_peer,
):
    gate, scale = mod[2:3, :], 1.0 + mod[4:5, :]
    for rows in blocks():
        resid, unused = resid_of(lat, mod, bias, part, part_recv, rows)
        normal, inverse = norm_of(resid)
        weighted = (grad_two[rows, :].astype(F32) + grad_two_recv[rows, :].astype(F32)) * scale
        back = inverse * (weighted - row_mean(weighted) - normal * row_mean(weighted * normal))
        grads = cot[rows, :].astype(F32) + back
        grad_resid[rows, :] = grads
        gated = (grads * gate).astype(BF16)
        grad_own[rows, :] = gated[:, :HALF]
        grad_peer[rows, :] = gated[:, HALF:]
    for h in range(HEADS):
        base = h * 192
        query, key = packed[base : base + 64, :], packed[base + 64 : base + 128, :]
        value = packed[base + 128 : base + 192, :]
        wide = slice(h * 64, h * 64 + 64)
        grad_att = mm(out_own[wide, :], grad_own[...], (1, 1)) + mm(out_peer[wide, :], grad_peer[...], (1, 1))
        grad_att = grad_att.astype(BF16)
        scores = mm(key, query, (0, 0)) * 0.125
        expon = jnp.exp(scores - jnp.max(scores, axis=0, keepdims=True))
        probs = expon * (1.0 / jnp.sum(expon, axis=0, keepdims=True))
        grad_probs = mm(value, grad_att, (0, 0))
        total = jnp.sum(probs * grad_probs, axis=0, keepdims=True)
        grad_scores = (probs * (grad_probs - total)).astype(BF16)
        grad_packed[base : base + 64, :] = (mm(key, grad_scores, (1, 0)) * 0.125).astype(BF16)
        grad_packed[base + 64 : base + 128, :] = (mm(query, grad_scores, (1, 1)) * 0.125).astype(BF16)
        grad_packed[base + 128 : base + 192, :] = mm(grad_att, probs.astype(BF16), (1, 1)).astype(BF16)
    grad_packed[QKV:, :] = grad_peer[...].T
    part_three[0:SEQ, :HALF] = mm(grad_packed[0:QKV, :], qkv_own[...], (0, 0)).astype(BF16)
    part_three[0:SEQ, HALF:] = mm(grad_packed[0:QKV, :], qkv_peer[...], (0, 0)).astype(BF16)
    values = sums[0:1, :]
    high = values.astype(BF16).astype(F32)
    middle = (values - high).astype(BF16).astype(F32)
    place = lax.broadcasted_iota(jnp.int32, (16, D), 0)
    terms = jnp.where(place == 0, high, jnp.where(place == 1, middle, jnp.where(place == 2, values - high - middle, 0.0)))
    part_three[SEQ : SEQ + 16, :] = terms.astype(BF16)


def proj_grad_kernel(
    left, bit, normed, normed_recv, packed, packed_recv, grad, attended, attended_recv,
    send, keep, out_bias, pack_bias,
):
    rows = tokens(normed, normed_recv)
    packs = jnp.concatenate([packed[0:QKV, :], packed_recv[0:QKV, :]], axis=1)
    grads = jnp.concatenate([grad[...].T, packed_recv[QKV:, :]], axis=1)
    atts = tokens(attended, attended_recv, 1)
    ones = jnp.ones((16, 2 * SEQ), BF16)
    out_bias[...] = mm(ones, grads, (1, 1))[0:1]
    sums = mm(ones, packs, (1, 1))[0:1]
    pack_bias[...] = jnp.where(lax.axis_index("col") == 0, sums[:, : QKV // 2], sums[:, QKV // 2 :])
    full = halves(mm(rows, packs, (0, 1)), mm(grads, atts, (1, 1)))
    split_store(full, left, bit, send, keep)


def last_kernel(
    lat, mod, bias, part, part_recv, grad_two, grad_two_recv, cot,
    grad_resid, grad_one, grad_one_recv, branch_sums,
    lat_own, lat_peer, mod_own, mod_peer,
):
    scale = 1.0 + mod[1:2, :]
    sums = [jnp.zeros((1, D), F32)] * 6
    for rows in blocks():
        resid, one = resid_of(lat, mod, bias, part, part_recv, rows)
        normal_two, unused = norm_of(resid)
        normal, inverse = norm_of(lat[rows, :].astype(F32))
        normed_grad = grad_one[rows, :].astype(F32) + grad_one_recv[rows, :].astype(F32)
        normed_two = grad_two[rows, :].astype(F32) + grad_two_recv[rows, :].astype(F32)
        resid_grad = grad_resid[rows, :]
        weighted = normed_grad * scale
        back = inverse * (weighted - row_mean(weighted) - normal * row_mean(weighted * normal))
        grads = resid_grad + back
        lat_own[rows, :] = grads[:, :HALF]
        lat_peer[rows, :] = grads[:, HALF:]
        terms = (
            normed_grad,
            normed_grad * normal,
            resid_grad * one,
            normed_two,
            normed_two * normal_two,
            cot[rows, :].astype(F32),
        )
        sums = [s + jnp.sum(t, axis=0, keepdims=True) for s, t in zip(sums, terms)]
    far = grad_one_recv[SEQ : SEQ + 16, :].astype(F32)
    far = far[0:1] + far[1:2] + far[2:3]
    sums[5] = sums[5] * bias[1:2, :] + branch_sums[0:1, :] + far
    for k in range(6):
        mod_own[k : k + 1, :] = sums[k][:, :HALF]
        mod_peer[k : k + 1, :] = sums[k][:, HALF:]


def out_kernel(lat, mod, bias, part, part_recv, part_two, part_two_recv, own, peer):
    for rows in blocks():
        resid, unused = resid_of(lat, mod, bias, part, part_recv, rows)
        two = branch(part_two, part_two_recv, bias[1:2, :], rows)
        result = (resid + mod[5:6, :] * two).astype(BF16)
        own[rows, :] = result[:, :HALF]
        peer[rows, :] = result[:, HALF:]


def payload_kernel(mod_own, mod_recv, soft, up_bias, down_bias, out_bias, pack_bias, payload):
    payload = payload.at[0]
    col_index = lax.axis_index("col")
    own, recv = mod_own[...], mod_recv[...]
    payload[...] = jnp.zeros(payload.shape, F32)
    payload[0:6, :] = jnp.where(col_index == 0, own, recv)
    payload[6:7, :] = soft[0:1, :]
    payload[8:14, :] = jnp.where(col_index == 0, recv, own)
    payload[14:15, :] = soft[1:2, :]
    for k in range(4):
        payload[16 + k : 17 + k, :] = up_bias[:, k * HALF : k * HALF + HALF]
    payload[20:21, :] = down_bias[...]
    payload[21:22, :] = out_bias[...]
    payload[22:23, :] = pack_bias[:, :HALF]
    payload[23:24, 0:192] = pack_bias[:, HALF:]


def cond_kernel(mod_own, mod_recv, weight, part_cond, mark):
    col_index = lax.axis_index("col")
    own, recv = mod_own[...], mod_recv[...]
    zero = jnp.where(col_index == 0, own, recv)
    one = jnp.where(col_index == 0, recv, own)
    place = lax.broadcasted_iota(jnp.int32, (16, HALF), 0)
    total = jnp.zeros((16, HALF), F32)
    for k in range(6):
        terms = jnp.zeros((16, HALF), F32)
        for i, row in enumerate((zero[k : k + 1], one[k : k + 1])):
            high = row.astype(BF16).astype(F32)
            middle = (row - high).astype(BF16).astype(F32)
            low = row - high - middle
            for j, term in enumerate((high, middle, low)):
                terms = jnp.where(place == 3 * i + j, term, terms)
        total = total + mm(terms.astype(BF16), weight[k], (1, 1))
    part_cond[0:1, :] = total[0:1] + total[1:2] + total[2:3]
    part_cond[1:2, :] = total[3:4] + total[4:5] + total[5:6]
    mark[...] = jnp.zeros(mark.shape, F32)


def finish_kernel(out_own, out_recv, lat_own, lat_recv, cond, part, part_recv, out, lat, grad_cond, mark):
    mark[...] = jnp.zeros(mark.shape, F32)
    same = lax.axis_index("row") == lax.axis_index("col")
    out[...] = jnp.where(same, out_own[...], out_recv[...])
    lat[...] = jnp.where(same, lat_own[...], lat_recv[...])
    values = cond[...]
    gate = 1.0 / (1.0 + jnp.exp(-values))
    grad_cond[...] = (part[...] + part_recv[...]) * (gate * (1.0 + values * (1.0 - gate)))


def add_kernel(left, bit, keep, recv, send_next, keep_next):
    here = bit_here(bit)
    step, places = spots(left, bit)
    for q, first in enumerate(places):
        for place, out in ((first + step * here, keep_next), (first + step * (1 - here), send_next)):
            out[q] = (keep[place].astype(F32) + recv[place].astype(F32)).astype(BF16)


def join_kernel(first, second, out):
    count = first.shape[0]
    out[0:count] = first[...]
    out[count : 2 * count] = second[...]


def sum_kernel(keep, recv, out, mark):
    out[...] = keep[0].astype(F32) + recv[0].astype(F32)
    mark[...] = jnp.zeros(mark.shape, F32)


def proj_sum_kernel(keep, recv, qkv, out):
    both = keep[0].astype(F32) + recv[0].astype(F32)
    for k in range(3 * HEADS):
        qkv[k] = both[:, k * HD : k * HD + HD]
    for h in range(HEADS):
        out[h] = both[:, QKV + h * HD : QKV + h * HD + HD]


def lanes(values, start, width):
    count = values.shape[1]
    rows = lax.broadcasted_iota(jnp.int32, (count, width), 0)
    columns = lax.broadcasted_iota(jnp.int32, (count, width), 1)
    return mm(values, (rows == columns + start).astype(F32), (1, 0), HIGH)


def mod_sum_kernel(loads, weight, mod_bias, up_bias, down_bias, out_bias, pack_bias, mark):
    shards = loads.shape[0]
    dp_index = lax.axis_index("dp")
    part = HALF // shards
    count = 2 * shards
    images = [loads[s, 8 * i : 8 * i + 8, :] for s in range(shards) for i in range(2)]
    soft = jnp.concatenate([image[6:7] for image in images], axis=0)
    rows = jnp.concatenate([image[k : k + 1] for k in range(6) for image in images], axis=0)
    rows = lanes(rows, dp_index * part, part)
    for k in range(6):
        here = rows[k * count : (k + 1) * count]
        mod_bias[k] = jnp.sum(here, axis=0, keepdims=True)
        weight[k] = mm(here, soft, (0, 0), HIGH)
    total = loads[0, 16:24, :]
    for s in range(1, shards):
        total = total + loads[s, 16:24, :]
    start = dp_index * (4 * part)
    row = lax.div(start, HALF)
    picked = jnp.where(lax.broadcasted_iota(jnp.int32, (8, HALF), 0) == row, total, 0.0)
    up_bias[...] = lanes(jnp.sum(picked, axis=0, keepdims=True), start - row * HALF, 4 * part)
    blocks_here = lanes(total, dp_index * part, part)
    down_bias[...] = blocks_here[4:5]
    out_bias[...] = blocks_here[5:6]
    heads = []
    for h in range(HEADS // 2):
        for i in range(2):
            row, spot = divmod(h * 192 + i * 128, HALF)
            heads.append(total[6 + row : 7 + row, spot : spot + HD])
    heads = lanes(jnp.concatenate(heads, axis=0), dp_index * (HD // shards), HD // shards)
    for h in range(HEADS // 2):
        pack_bias[h] = heads[2 * h : 2 * h + 2]
    mark[...] = jnp.zeros(mark.shape, F32)


def row_swap(values):
    return lax.ppermute(values, "row", SWAP)


def col_swap(values):
    return lax.ppermute(values, "col", SWAP)


def both_swap(values):
    return lax.ppermute(values, ("row", "col"), [(0, 3), (3, 0), (1, 2), (2, 1)])


def swap_bit(values, bit, dp_size):
    return lax.ppermute(values, "dp", [(p, p ^ (1 << bit)) for p in range(dp_size)])


class Sums:
    def __init__(self, name, order, dp_size):
        self.name, self.order, self.dp_size = name, order, dp_size
        self.left, self.step = tuple(sorted(order, reverse=True)), 0

    def exchange(self, send, keep, after=()):
        if after:
            send = lax.optimization_barrier((send, *after))[0]
        self.keep, self.recv = keep, swap_bit(send, self.order[self.step], self.dp_size)

    def add(self, after, micros=0.5):
        self.left = tuple(b for b in self.left if b != self.order[self.step])
        self.step += 1
        shape = (self.keep.shape[0] // 2,) + self.keep.shape[1:]
        kernel = functools.partial(add_kernel, self.left, self.order[self.step])
        return call(kernel, [(shape, BF16)] * 2, [self.keep, self.recv], micros, self.name, after)

    def advance(self, after, micros=0.5):
        if self.step + 1 >= len(self.order):
            return after[0]
        send, keep = self.add(after, micros)
        self.exchange(send, keep)
        return keep

    def finish(self, kernel, outs, after, micros=0.5):
        return call(kernel, outs, [self.keep, self.recv], micros, self.name + "_sum", after)


def shards_fn(
    dp_size,
    latents,
    labels,
    timesteps,
    class_table,
    mod_weight,
    mod_bias,
    qkv_weight,
    query_value_bias,
    out_weight,
    out_bias,
    up_weight,
    up_bias,
    down_weight,
    down_bias,
    cotangent,
):
    bits = dp_size.bit_length() - 1
    wide = (SEQ, D)
    slim = (SEQ, HALF)
    pieces = dp_size // 2
    rows_down, rows_up = HALF // dp_size, FEED // dp_size
    every = tuple(range(bits))
    left = every[::-1]
    up = Sums("up_add", every[1:2] + every[:1] + every[2:], dp_size)
    down = Sums("down_add", every[:1] + every[2:] + every[1:2], dp_size)
    proj = Sums("proj_add", every, dp_size)
    change = [(1, 2), (2, 1)]
    classes = class_table.shape[0]
    picks = (labels[:, None] == jnp.arange(classes, dtype=jnp.int32)[None, :]).astype(BF16)
    looked = jnp.dot(picks, class_table, preferred_element_type=F32)
    change = [(1, 2), (2, 1)]
    lat_col = col_swap(latents)
    cot_col = col_swap(cotangent)
    qkv_own = jnp.transpose(qkv_weight, (1, 2, 3, 0)).reshape(QKV, HALF)
    out_own = out_weight.reshape(HALF, HALF)
    qkv_peer, out_peer = col_swap(qkv_own), col_swap(out_own)

    frequency = jnp.exp(-math.log(10000.0) * jnp.arange(HALF, dtype=F32) / HALF)
    angles = timesteps.astype(F32)[:, None] * frequency[None, :]
    mod_rows = jnp.transpose(mod_weight, (1, 0, 2))
    mod_part, soft, cond = call(
        mod_kernel,
        [((16, HALF), F32), ((2, HALF), F32), ((2, HALF), F32)],
        [looked, jnp.cos(angles), jnp.sin(angles), mod_rows],
        20,
        "mod",
        [looked],
    )
    mod_part_recv = row_swap(mod_part)
    (lat_both,) = call(pack_kernel, [((2 * SEQ, HALF), BF16)], [latents, lat_col], 0.4, "pack", [mod_part])
    lat_change = lax.ppermute(lat_both, ("row", "col"), change)
    (cot_both,) = call(pack_kernel, [((2 * SEQ, HALF), BF16)], [cotangent, cot_col], 0.4, "pack", [lat_both])
    cot_change = lax.ppermute(cot_both, ("row", "col"), change)
    keep, other = call(
        mix_kernel,
        [((6, HALF), F32), ((16, HALF), F32)],
        [mod_part, mod_part_recv, mod_bias, out_bias, down_bias, query_value_bias],
        0.1,
        "mix",
        [cot_both, qkv_peer, out_peer],
    )
    other_col = col_swap(other)
    lat, normal = call(
        norm_kernel, [(wide, BF16), (wide, F32)], [latents, lat_col, lat_change], 1.8, "norm", [keep]
    )
    up_weight, down_weight = lax.optimization_barrier((up_weight, down_weight, other_col))[:2]
    down_peer, up_peer = col_swap(down_weight), col_swap(up_weight)
    mod, bias, normed_own, normed_peer, packed, attended, part_one = call(
        first_kernel,
        [((6, D), F32), ((8, D), F32), (slim, BF16), (slim, BF16), ((QKV, SEQ), BF16), ((HALF, SEQ), BF16), (wide, BF16)],
        [normal, keep, other, other_col, qkv_own, qkv_peer, out_own, out_peer],
        5,
        "first",
    )
    part_one_recv = row_swap(part_one)
    cot, two_grad_own, two_grad_peer, grad_active = call(
        early_kernel,
        [(wide, BF16), (slim, BF16), (slim, BF16), ((SEQ, FEED), F32)],
        [cotangent, cot_col, cot_change, mod, down_weight, down_peer],
        1,
        "early",
        [part_one],
    )
    normed_recv, attended_recv = col_swap(normed_peer), col_swap(attended)
    two_grad_recv = col_swap(two_grad_peer)
    resid_args = [lat, mod, bias, part_one, part_one_recv]
    second_own, active, hidden, part_two = call(
        second_kernel,
        [(slim, BF16), ((SEQ, FEED), BF16), ((SEQ, FEED + HALF), BF16), (wide, BF16)],
        [*resid_args, up_weight, up_peer, up_bias, grad_active],
        4,
        "second",
        [normed_recv, attended_recv, two_grad_recv],
    )
    part_two_recv = row_swap(part_two)
    active_recv, hidden_recv = col_swap(active), col_swap(hidden)
    branch_part, branch_sums = call(
        down_kernel, [(wide, BF16), ((8, D), F32)], [active, cot, down_weight, down_peer], 1, "down"
    )
    branch_recv = lax.ppermute(branch_part, ("row", "col"), [(1, 3), (2, 0)])
    down_send, down_keep, down_sum = call(
        functools.partial(down_grad_kernel, left, down.order[0]),
        [((pieces, rows_down, FEED), BF16), ((pieces, rows_down, FEED), BF16), ((1, HALF), F32)],
        [two_grad_own, two_grad_recv, active, active_recv],
        0.9,
        "down_grad",
        [branch_part],
    )
    down.exchange(down_send, down_keep)
    up_send, up_keep, up_sum = call(
        functools.partial(up_grad_kernel, left, up.order[0]),
        [((pieces, rows_up, HALF), BF16), ((pieces, rows_up, HALF), BF16), ((1, FEED), F32)],
        [second_own, hidden, hidden_recv],
        1.2,
        "up_grad",
        [down_send],
    )
    up.exchange(up_send, up_keep)
    grad_resid, one_grad_own, grad_packed, part_three = call(
        third_kernel,
        [(wide, F32), (slim, BF16), ((QKV + HALF, SEQ), BF16), ((SEQ + 16, D), BF16)],
        [*resid_args, part_two, part_two_recv, cot, packed, branch_sums, qkv_own, qkv_peer, out_own, out_peer],
        20,
        "third",
        [up_send],
        [pltpu.VMEM(slim, BF16)],
    )
    part_three_recv = row_swap(part_three)
    packed_recv = col_swap(grad_packed)
    token = down.advance([part_three], 6)
    token = up.advance([token], 6)
    proj_send, proj_keep, out_sum, pack_sum = call(
        functools.partial(proj_grad_kernel, left, proj.order[0]),
        [
            ((pieces, rows_down, FEED), BF16),
            ((pieces, rows_down, FEED), BF16),
            ((1, HALF), F32),
            ((1, QKV // 2), F32),
        ],
        [normed_own, normed_recv, grad_packed, packed_recv, one_grad_own, attended, attended_recv],
        1.3,
        "proj_grad",
        [token],
    )
    proj.exchange(proj_send, proj_keep)
    token = proj_send
    lat_grad_own, lat_grad_peer, mod_own, mod_peer = call(
        last_kernel,
        [(slim, F32), (slim, F32), ((6, HALF), F32), ((6, HALF), F32)],
        [*resid_args, part_two, part_two_recv, cot, grad_resid, part_three, part_three_recv, branch_sums],
        20,
        "last",
        [token],
    )
    mod_recv = col_swap(mod_peer)
    token = down.advance([mod_own])
    token = up.advance([token], 3)
    (payload,) = call(
        payload_kernel,
        [((1, 24, HALF), F32)],
        [mod_own, mod_recv, soft, up_sum, down_sum, out_sum, pack_sum],
        0.01,
        "payload",
        [token],
    )
    result_own, result_peer = call(
        out_kernel,
        [(slim, BF16), (slim, BF16)],
        [*resid_args, branch_part, branch_recv],
        0.1,
        "out",
        [payload],
    )
    result_recv = col_swap(result_peer)
    lat_recv = col_swap(lax.optimization_barrier((lat_grad_peer, result_own))[0])
    token = result_own
    mark = ((8, 128), F32)
    for step, bit in enumerate(every[::-1]):
        recv = swap_bit(payload, bit, dp_size)
        if step == 1:
            token = proj.advance([token], 20)
            while min(down.step, up.step) + 1 < bits:
                for part in (down, up):
                    token = part.advance([token], 0.1)
            token = proj.advance([token], 0.1)
        if step == 2:
            down_grad, token = down.finish(sum_kernel, [((rows_down, FEED), F32), mark], [token], 0.1)
            up_grad, token = up.finish(sum_kernel, [((rows_up, HALF), F32), mark], [token], 0.1)
        (payload,) = call(join_kernel, [((2 << step, 24, HALF), F32)], [payload, recv], 0.1, "join", [token])
        token = payload
    while proj.step + 1 < bits:
        token = proj.advance([token])
    width = HALF // dp_size
    mod_grad, mod_bias_grad, up_bias_grad, down_bias_grad, out_bias_grad, pack_grad, mod_mark = call(
        mod_sum_kernel,
        [
            ((6, width, HALF), F32),
            ((6, 1, width), F32),
            ((1, rows_up), F32),
            ((1, width), F32),
            ((1, width), F32),
            ((HEADS // 2, 2, HD // dp_size), F32),
            mark,
        ],
        [payload],
        0.1,
        "mod_sum",
        [token],
    )
    part_cond, part_cond_mark = call(
        cond_kernel, [((2, HALF), F32), mark], [mod_own, mod_recv, mod_rows], 0.1, "cond", [mod_mark]
    )
    output, grad_latents, grad_cond, finish_mark = call(
        finish_kernel,
        [(slim, BF16), (slim, F32), ((2, HALF), F32), mark],
        [result_own, result_recv, lat_grad_own, lat_recv, cond, part_cond, col_swap(part_cond)],
        0.5,
        "finish",
    )
    qkv_grad, out_grad = proj.finish(
        proj_sum_kernel,
        [((3 * HEADS, rows_down, HD), F32), ((HEADS, rows_down, HD), F32)],
        [finish_mark],
    )
    return (
        output,
        grad_latents,
        grad_cond,
        jnp.transpose(mod_grad, (2, 0, 1))[:, :, None, :],
        mod_bias_grad,
        jnp.transpose(qkv_grad.reshape(HEADS, 3, rows_down, HD), (2, 0, 1, 3))[None],
        jnp.transpose(pack_grad, (1, 0, 2)),
        jnp.transpose(out_grad, (0, 2, 1))[:, :, None, :],
        out_bias_grad,
        jnp.transpose(up_grad)[:, None, :],
        up_bias_grad,
        jnp.transpose(down_grad)[:, None, :],
        down_bias_grad,
    )


def solution(mesh):
    in_specs = (
        P(("dp", "row"), "col"),
        P("dp"),
        P("dp"),
        P(None, "row"),
        P("row", None, "col"),
        P(None, "col"),
        P("col", "row", None, None),
        P(None, ("row", "col"), None),
        P("row", None, "col"),
        P("col"),
        P("col", "row"),
        P("row"),
        P("row", "col"),
        P("col"),
        P(("dp", "row"), "col"),
    )
    out_specs = (
        P(("dp", "row"), "col"),
        P(("dp", "row"), "col"),
        P("dp", "row"),
        P("row", None, "col", "dp"),
        P(None, "col", "dp"),
        P("col", "dp", "row", None, None),
        P(None, ("row", "col"), "dp"),
        P("row", None, "col", "dp"),
        P("col", "dp"),
        P("col", "row", "dp"),
        P("row", "dp"),
        P("row", "col", "dp"),
        P("col", "dp"),
    )
    body = functools.partial(shards_fn, mesh.shape["dp"])
    return jax.shard_map(body, mesh=mesh, in_specs=in_specs, out_specs=out_specs, check_vma=False)
```

profile of v0, /device:TPU:0, one launch (start us, length us, event | category | flops | bytes accessed | tf_op | source)
XLA Modules:
  0.0 108.5 jit_solution(4827221309520805861)
XLA Ops:
  3.5 1.5 %copy-done.1 = bf16[384,6,384]{2,0,1:T(8,128)(2,1)S(1)} copy-done((bf16[384,6,384]{2,0,1:T(8,128)(2,1)S(1)}, bf16[384,6,384]{2,0,1:T(8,128)(2,1)}, u32[]{:S(2)}) %copy-start.1) | copy-done | bytes 1769496
  5.4 3.0 %collective-permute-start.4 = (f32[16,384]{1,0:T(8,128)S(1)}, f32[16,384]{1,0:T(8,128)S(1)}, u32[]{:S(2)}, u32[]{:S(2)}) collective-permute-start(f32[16,384]{1,0:T(8,128)S(1)} %get-tuple-element.90.refs_0_.refs_3_), channel_id=1, source_target_pairs={{0,2},{2,0},{1,3},{3,1},{4,6},{6,4},{5,7},{7,5},{8,10},{10,8},{9,1... | collective-permute-start | bytes 73736 | tf_op jit(solution)/shard_map/ppermute | solution.py:476
  10.3 1.1 collective-permute-start.6
  14.7 4.8 %first.1 = (f32[6,768]{1,0:T(8,128)S(1)}, f32[8,768]{1,0:T(8,128)S(1)}, bf16[256,384]{1,0:T(8,128)(2,1)S(1)}, bf16[256,384]{1,0:T(8,128)(2,1)S(1)}, bf16[1152,25...) custom-call(f32[256,768]{1,0:T(8,128)S(1)} %get-tuple-element.92.normal, ...), custom_call_target="tpu_custom_call" | custom-call | flops 5750000128 | bytes 1024 | tf_op jit(solution)/shard_map/first/pallas_call | solution.py:39
  19.5 4.8 %collective-permute-start.12 = (bf16[256,768]{1,0:T(8,128)(2,1)S(1)}, bf16[256,768]{1,0:T(8,128)(2,1)S(1)}, u32[]{:S(2)}, u32[]{:S(2)}) collective-permute-start(bf16[256,768]{1,0:T(8,128)(2,1)S(1)} %get-tuple-element.96.refs_0_.refs_6_.refs_4_), channel_id=1, source_target_pairs={{0,2},{2,0},{1,3},{3,1},{4,6},{6,4},{5,7},{7,5},{8,10},{10,8},{9,1... | collective-permute-start | bytes 1179656 | tf_op jit(solution)/shard_map/ppermute | solution.py:476
  26.0 8.0 %collective-permute-done.12.refs_7_.refs_5_ = bf16[256,768]{1,0:T(8,128)(2,1)S(1)} collective-permute-done((bf16[256,768]{1,0:T(8,128)(2,1)S(1)}, bf16[256,768]{1,0:T(8,128)(2,1)S(1)}, u32[]{:S(2)}, u32[]{:S(2)}) %collective-permute-start.12) | collective-permute-done | bytes 393248 | tf_op jit(solution)/shard_map/ppermute | solution.py:476
  34.0 3.0 %second.1 = (bf16[256,384]{1,0:T(8,128)(2,1)S(1)}, bf16[256,1536]{1,0:T(8,128)(2,1)S(1)}, bf16[256,1920]{1,0:T(8,128)(2,1)S(1)}, bf16[256,768]{1,0:T(8,128)(2,1)S(1)}) custom-call(bf16[256,384]{1,0:T(8,128)(2,1)S(1)} %collective-permute-done.7.refs_0_.refs_2_, bf16[384,256]{1,0:T(8,128)(2,1)S(1)} %collective-permute-done.8.refs_1_.refs_7_, ...), custom_call_target="tpu_custom_call" | custom-call | flops 4600000000 | bytes 1024 | tf_op jit(solution)/shard_map/second/pallas_call | solution.py:39
  39.5 1.5 %collective-permute-start.24 = (bf16[256,768]{1,0:T(8,128)(2,1)S(1)}, bf16[256,768]{1,0:T(8,128)(2,1)S(1)}, u32[]{:S(2)}, u32[]{:S(2)}) collective-permute-start(bf16[256,768]{1,0:T(8,128)(2,1)S(1)} %get-tuple-element.106.refs_0_.refs_6_), channel_id=1, source_target_pairs={{1,3},{2,0},{5,7},{6,4},{9,11},{10,8},{13,15},{14,12},{17,19},{18,... | collective-permute-start | bytes 1179656 | tf_op jit(solution)/shard_map/ppermute | solution.py:620
  41.8 1.6 %collective-permute-start.17 = (bf16[4,48,1536]{2,1,0:T(8,128)(2,1)S(1)}, bf16[4,48,1536]{2,1,0:T(8,128)(2,1)S(1)}, u32[]{:S(2)}, u32[]{:S(2)}) collective-permute-start(bf16[4,48,1536]{2,1,0:T(8,128)(2,1)S(1)} %get-tuple-element.108.refs_0_), channel_id=1, source_target_pairs={{0,4},{4,0},{8,12},{12,8},{16,20},{20,16},{24,28},{28,24},{1,5},{5... | collective-permute-start | bytes 1769480 | tf_op jit(solution)/shard_map/ppermute | solution.py:488
  43.4 1.2 %up_grad.1 = (bf16[4,192,384]{2,1,0:T(8,128)(2,1)S(1)}, bf16[4,192,384]{2,1,0:T(8,128)(2,1)S(1)}, f32[1,1536]{1,0:T(1,128)S(1)}) custom-call(bf16[4,48,1536]{2,1,0:T(8,128)(2,1)S(1)} %get-tuple-element.108.refs_0_, bf16[256,384]{1,0:T(8,128)(2,1)S(1)} %get-tuple-element.109.refs_1_, bf16[256,1920]{1,0:T(8,128)(2,1)S(1)} %get-tuple-element.110.refs_2_, ...), custom_call_target="tpu_custom_call" | custom-call | flops 1380000000 | bytes 1024 | tf_op jit(solution)/shard_map/up_grad/pallas_call | solution.py:39
  44.6 1.6 %collective-permute-start.18 = (bf16[4,192,384]{2,1,0:T(8,128)(2,1)S(1)}, bf16[4,192,384]{2,1,0:T(8,128)(2,1)S(1)}, u32[]{:S(2)}, u32[]{:S(2)}) collective-permute-start(bf16[4,192,384]{2,1,0:T(8,128)(2,1)S(1)} %get-tuple-element.111.refs_0_), channel_id=1, source_target_pairs={{0,8},{4,12},{8,0},{12,4},{16,24},{20,28},{24,16},{28,20},{1,9},{5... | collective-permute-start | bytes 1769480 | tf_op jit(solution)/shard_map/ppermute | solution.py:488
  46.2 2.4 %collective-permute-done.16.refs_7_ = bf16[256,768]{1,0:T(8,128)(2,1)S(1)} collective-permute-done((bf16[256,768]{1,0:T(8,128)(2,1)S(1)}, bf16[256,768]{1,0:T(8,128)(2,1)S(1)}, u32[]{:S(2)}, u32[]{:S(2)}) %collective-permute-start.16) | collective-permute-done | bytes 393248 | tf_op jit(solution)/shard_map/ppermute | solution.py:476
  48.6 5.5 %third.1 = (f32[256,768]{1,0:T(8,128)S(1)}, bf16[256,384]{1,0:T(8,128)(2,1)S(1)}, bf16[1536,256]{1,0:T(8,128)(2,1)S(1)}, bf16[272,768]{1,0:T(8,128)(2,1)S(1)}) custom-call(bf16[4,192,384]{2,1,0:T(8,128)(2,1)S(1)} %get-tuple-element.111.refs_0_, bf16[256,768]{1,0:T(8,128)(2,1)S(1)} %get-tuple-element.100.refs_3_.refs_1_, ...), custom_call_target="tpu_custom_call" | custom-call | flops 23000000512 | bytes 1024 | tf_op jit(solution)/shard_map/third/pallas_call | solution.py:39
  54.2 1.9 %collective-permute-start.20 = (bf16[272,768]{1,0:T(8,128)(2,1)S(1)}, bf16[272,768]{1,0:T(8,128)(2,1)S(1)}, u32[]{:S(2)}, u32[]{:S(2)}) collective-permute-start(bf16[272,768]{1,0:T(8,128)(2,1)S(1)} %get-tuple-element.115.refs_0_.refs_10_), channel_id=1, source_target_pairs={{0,2},{2,0},{1,3},{3,1},{4,6},{6,4},{5,7},{7,5},{8,10},{10,8},{9,1... | collective-permute-start | bytes 1253384 | tf_op jit(solution)/shard_map/ppermute | solution.py:476
  56.1 1.7 %collective-permute-done.17.refs_2_ = bf16[4,48,1536]{2,1,0:T(8,128)(2,1)S(1)} collective-permute-done((bf16[4,48,1536]{2,1,0:T(8,128)(2,1)S(1)}, bf16[4,48,1536]{2,1,0:T(8,128)(2,1)S(1)}, u32[]{:S(2)}, u32[]{:S(2)}) %collective-permute-start.17) | collective-permute-done | bytes 589856 | tf_op jit(solution)/shard_map/ppermute | solution.py:488
  57.9 2.6 %collective-permute-start.21 = (bf16[2,48,1536]{2,1,0:T(8,128)(2,1)S(1)}, bf16[2,48,1536]{2,1,0:T(8,128)(2,1)S(1)}, u32[]{:S(2)}, u32[]{:S(2)}) collective-permute-start(bf16[2,48,1536]{2,1,0:T(8,128)(2,1)S(1)} %get-tuple-element.126), channel_id=1, source_target_pairs={{0,16},{4,20},{8,24},{12,28},{16,0},{20,4},{24,8},{28,12},{1,17},{... | collective-permute-start | bytes 884744 | tf_op jit(solution)/shard_map/ppermute | solution.py:488
  61.0 1.3 %collective-permute-start.22 = (bf16[2,192,384]{2,1,0:T(8,128)(2,1)S(1)}, bf16[2,192,384]{2,1,0:T(8,128)(2,1)S(1)}, u32[]{:S(2)}, u32[]{:S(2)}) collective-permute-start(bf16[2,192,384]{2,1,0:T(8,128)(2,1)S(1)} %get-tuple-element.128), channel_id=1, source_target_pairs={{0,4},{4,0},{8,12},{12,8},{16,20},{20,16},{24,28},{28,24},{1,5},{5... | collective-permute-start | bytes 884744 | tf_op jit(solution)/shard_map/ppermute | solution.py:488
  62.3 1.4 %proj_grad.1 = (bf16[4,48,1536]{2,1,0:T(8,128)(2,1)S(1)}, bf16[4,48,1536]{2,1,0:T(8,128)(2,1)S(1)}, f32[1,384]{1,0:T(1,128)S(1)}, f32[1,576]{1,0:T(1,128)S(1)}) custom-call(bf16[2,192,384]{2,1,0:T(8,128)(2,1)S(1)} %get-tuple-element.119.refs_0_.refs_1_, bf16[256,384]{1,0:T(8,128)(2,1)S(1)} %get-tuple-element.120.refs_1_, ...), custom_call_target="tpu_custom_call" | custom-call | flops 1495000064 | bytes 1024 | tf_op jit(solution)/shard_map/proj_grad/pallas_call | solution.py:39
  64.5 1.8 %collective-permute-done.20.refs_11_ = bf16[272,768]{1,0:T(8,128)(2,1)S(1)} collective-permute-done((bf16[272,768]{1,0:T(8,128)(2,1)S(1)}, bf16[272,768]{1,0:T(8,128)(2,1)S(1)}, u32[]{:S(2)}, u32[]{:S(2)}) %collective-permute-start.20) | collective-permute-done | bytes 417824 | tf_op jit(solution)/shard_map/ppermute | solution.py:476
  66.3 1.3 %last.1 = (f32[256,384]{1,0:T(8,128)S(1)}, f32[256,384]{1,0:T(8,128)S(1)}, f32[6,384]{1,0:T(8,128)S(1)}, f32[6,384]{1,0:T(8,128)S(1)}) custom-call(bf16[4,48,1536]{2,1,0:T(8,128)(2,1)S(1)} %get-tuple-element.123.refs_0_, bf16[256,768]{1,0:T(8,128)(2,1)S(1)} %get-tuple-element.100.refs_3_.refs_1_, f32[6,768]{1,0:T(8,128)S(1)} %get-tuple-element.97.refs_4_.refs_2_, ...), custom_call_target="tpu_custom_call" | custom-call | flops 23000000512 | bytes 1024 | tf_op jit(solution)/shard_map/last/pallas_call | solution.py:39
  67.7 6.8 %collective-permute-done.21.refs_2_ = bf16[2,48,1536]{2,1,0:T(8,128)(2,1)S(1)} collective-permute-done((bf16[2,48,1536]{2,1,0:T(8,128)(2,1)S(1)}, bf16[2,48,1536]{2,1,0:T(8,128)(2,1)S(1)}, u32[]{:S(2)}, u32[]{:S(2)}) %collective-permute-start.21) | collective-permute-done | bytes 294944 | tf_op jit(solution)/shard_map/ppermute | solution.py:488
  75.2 5.2 %collective-permute-done.27.refs_2_ = f32[1,24,384]{2,1,0:T(8,128)S(1)} collective-permute-done((f32[1,24,384]{2,1,0:T(8,128)S(1)}, f32[1,24,384]{2,1,0:T(8,128)S(1)}, u32[]{:S(2)}, u32[]{:S(2)}) %collective-permute-start.27) | collective-permute-done | bytes 36896 | tf_op jit(solution)/shard_map/ppermute | solution.py:488
  80.4 2.3 %collective-permute-done.28.refs_2_ = bf16[4,48,1536]{2,1,0:T(8,128)(2,1)S(1)} collective-permute-done((bf16[4,48,1536]{2,1,0:T(8,128)(2,1)S(1)}, bf16[4,48,1536]{2,1,0:T(8,128)(2,1)S(1)}, u32[]{:S(2)}, u32[]{:S(2)}) %collective-permute-start.28) | collective-permute-done | bytes 589856 | tf_op jit(solution)/shard_map/ppermute | solution.py:488
  82.9 1.6 %collective-permute-start.29 = (bf16[2,48,1536]{2,1,0:T(8,128)(2,1)S(1)}, bf16[2,48,1536]{2,1,0:T(8,128)(2,1)S(1)}, u32[]{:S(2)}, u32[]{:S(2)}) collective-permute-start(bf16[2,48,1536]{2,1,0:T(8,128)(2,1)S(1)} %get-tuple-element.144), channel_id=1, source_target_pairs={{0,8},{4,12},{8,0},{12,4},{16,24},{20,28},{24,16},{28,20},{1,9},{5... | collective-permute-start | bytes 884744 | tf_op jit(solution)/shard_map/ppermute | solution.py:488
  85.0 1.6 %collective-permute-start.31 = (bf16[1,48,1536]{2,1,0:T(8,128)(2,1)S(1)}, bf16[1,48,1536]{2,1,0:T(8,128)(2,1)S(1)}, u32[]{:S(2)}, u32[]{:S(2)}) collective-permute-start(bf16[1,48,1536]{2,1,0:T(8,128)(2,1)S(1)} %get-tuple-element.146), channel_id=1, source_target_pairs={{0,8},{4,12},{8,0},{12,4},{16,24},{20,28},{24,16},{28,20},{1,9},{5... | collective-permute-start | bytes 442376 | tf_op jit(solution)/shard_map/ppermute | solution.py:488
  86.6 2.6 %collective-permute-start.32 = (bf16[1,192,384]{2,1,0:T(8,128)(2,1)S(1)}, bf16[1,192,384]{2,1,0:T(8,128)(2,1)S(1)}, u32[]{:S(2)}, u32[]{:S(2)}) collective-permute-start(bf16[1,192,384]{2,1,0:T(8,128)(2,1)S(1)} %get-tuple-element.148), channel_id=1, source_target_pairs={{0,16},{4,20},{8,24},{12,28},{16,0},{20,4},{24,8},{28,12},{1,17},{... | collective-permute-start | bytes 442376 | tf_op jit(solution)/shard_map/ppermute | solution.py:488
  89.1 6.9 %collective-permute-done.29.refs_2_ = bf16[2,48,1536]{2,1,0:T(8,128)(2,1)S(1)} collective-permute-done((bf16[2,48,1536]{2,1,0:T(8,128)(2,1)S(1)}, bf16[2,48,1536]{2,1,0:T(8,128)(2,1)S(1)}, u32[]{:S(2)}, u32[]{:S(2)}) %collective-permute-start.29) | collective-permute-done | bytes 294944 | tf_op jit(solution)/shard_map/ppermute | solution.py:488
  96.1 1.4 %collective-permute-done.30.refs_2_ = f32[2,24,384]{2,1,0:T(8,128)S(1)} collective-permute-done((f32[2,24,384]{2,1,0:T(8,128)S(1)}, f32[2,24,384]{2,1,0:T(8,128)S(1)}, u32[]{:S(2)}, u32[]{:S(2)}) %collective-permute-start.30) | collective-permute-done | bytes 73760 | tf_op jit(solution)/shard_map/ppermute | solution.py:488
  97.5 1.3 %collective-permute-start.33 = (f32[4,24,384]{2,1,0:T(8,128)S(1)}, f32[4,24,384]{2,1,0:T(8,128)S(1)}, u32[]{:S(2)}, u32[]{:S(2)}) collective-permute-start(f32[4,24,384]{2,1,0:T(8,128)S(1)} %join.4.refs_0_.refs_1_), channel_id=1, source_target_pairs={{0,4},{4,0},{8,12},{12,8},{16,20},{20,16},{24,28},{28,24},{1,5},{5... | collective-permute-start | bytes 442376 | tf_op jit(solution)/shard_map/ppermute | solution.py:488
  99.1 1.7 %collective-permute-start.35 = (bf16[1,48,1536]{2,1,0:T(8,128)(2,1)S(1)}, bf16[1,48,1536]{2,1,0:T(8,128)(2,1)S(1)}, u32[]{:S(2)}, u32[]{:S(2)}) collective-permute-start(bf16[1,48,1536]{2,1,0:T(8,128)(2,1)S(1)} %get-tuple-element.158), channel_id=1, source_target_pairs={{0,16},{4,20},{8,24},{12,28},{16,0},{20,4},{24,8},{28,12},{1,17},{... | collective-permute-start | bytes 442376 | tf_op jit(solution)/shard_map/ppermute | solution.py:488
  102.8 1.9 %mod_sum.1 = (f32[6,48,384]{2,1,0:T(8,128)}, f32[6,1,48]{2,1,0:T(1,128)}, f32[1,192]{1,0:T(1,128)}, f32[1,48]{1,0:T(1,128)}, f32[1,48]{1,0:T(1,128)}, /*index=5*/f32[3,2,8]{2,1,0:T(2,128)}, f32[8,128]{1,0:T(8,128)S(1)}) custom-call(f32[8,24,384]{2,1,0:T(8,128)S(1)} %join.5.refs_0_.refs_1_, f32[8,24,384]{2,1,0:T(8,128)S(1)} %join.5.refs_0_.refs_1_), custom_call_target="tpu_custom_call" | custom-call | flops 115000000 | bytes 1024 | tf_op jit(solution)/shard_map/mod_sum/pallas_call | solution.py:39
  105.5 1.2 %collective-permute-done.34.part_recv = f32[2,384]{1,0:T(2,128)S(1)} collective-permute-done((f32[2,384]{1,0:T(2,128)S(1)}, f32[2,384]{1,0:T(2,128)S(1)}, u32[]{:S(2)}, u32[]{:S(2)}) %collective-permute-start.34) | collective-permute-done | bytes 3104 | tf_op jit(solution)/shard_map/ppermute | solution.py:480
  (104 shorter events, 21.1 us)
Async XLA Ops:
  0.7 7.7 %collective-permute-start = (bf16[256,384]{1,0:T(8,128)(2,1)}, bf16[256,384]{1,0:T(8,128)(2,1)S(1)}, u32[]{:S(2)}, u32[]{:S(2)}) collective-permute-start(bf16[256,384]{1,0:T(8,128)(2,1)} %refs_1_.6), channel_id=1, source_target_pairs={{0,1},{1,0},{2,3},{3,2},{4,5},{5,4},{6,7},{7,6},{8,9},{9,8},{10,11... | collective-permute-start | bytes 589832 | tf_op jit(solution)/shard_map/ppermute | solution.py:480
  1.2 8.1 %collective-permute-start.1 = (bf16[256,384]{1,0:T(8,128)(2,1)}, bf16[256,384]{1,0:T(8,128)(2,1)S(1)}, u32[]{:S(2)}, u32[]{:S(2)}) collective-permute-start(bf16[256,384]{1,0:T(8,128)(2,1)} %refs_1_.7), channel_id=1, source_target_pairs={{0,1},{1,0},{2,3},{3,2},{4,5},{5,4},{6,7},{7,6},{8,9},{9,8},{10,11... | collective-permute-start | bytes 589832 | tf_op jit(solution)/shard_map/ppermute | solution.py:480
  1.3 8.9 %collective-permute-start.2 = (bf16[1152,384]{1,0:T(8,128)(2,1)}, bf16[1152,384]{1,0:T(8,128)(2,1)S(1)}, u32[]{:S(2)}, u32[]{:S(2)}) collective-permute-start(bf16[1152,384]{1,0:T(8,128)(2,1)} %bitcast.30), channel_id=1, source_target_pairs={{0,1},{1,0},{2,3},{3,2},{4,5},{5,4},{6,7},{7,6},{8,9},{9,8},{10,11... | collective-permute-start | bytes 2654216 | tf_op jit(solution)/shard_map/ppermute | solution.py:480
  1.7 8.5 %collective-permute-start.3 = (bf16[384,384]{1,0:T(8,128)(2,1)}, bf16[384,384]{1,0:T(8,128)(2,1)S(1)}, u32[]{:S(2)}, u32[]{:S(2)}) collective-permute-start(bf16[384,384]{1,0:T(8,128)(2,1)} %bitcast.33), channel_id=1, source_target_pairs={{0,1},{1,0},{2,3},{3,2},{4,5},{5,4},{6,7},{7,6},{8,9},{9,8},{10,11... | collective-permute-start | bytes 884744 | tf_op jit(solution)/shard_map/ppermute | solution.py:480
  5.4 4.8 %collective-permute-start.4 = (f32[16,384]{1,0:T(8,128)S(1)}, f32[16,384]{1,0:T(8,128)S(1)}, u32[]{:S(2)}, u32[]{:S(2)}) collective-permute-start(f32[16,384]{1,0:T(8,128)S(1)} %get-tuple-element.90.refs_0_.refs_3_), channel_id=1, source_target_pairs={{0,2},{2,0},{1,3},{3,1},{4,6},{6,4},{5,7},{7,5},{8,10},{10,8},{9,1... | collective-permute-start | bytes 73736 | tf_op jit(solution)/shard_map/ppermute | solution.py:476
  8.5 5.0 %collective-permute-start.5 = (bf16[512,384]{1,0:T(8,128)(2,1)S(1)}, bf16[512,384]{1,0:T(8,128)(2,1)S(1)}, u32[]{:S(2)}, u32[]{:S(2)}) collective-permute-start(bf16[512,384]{1,0:T(8,128)(2,1)S(1)} %pack.2.refs_0_), channel_id=1, source_target_pairs={{1,2},{2,1},{5,6},{6,5},{9,10},{10,9},{13,14},{14,13},{17,18},{18,... | collective-permute-start | bytes 1179656 | tf_op jit(solution)/shard_map/ppermute | solution.py:571
  12.2 12.6 %collective-permute-start.10 = (bf16[1536,384]{1,0:T(8,128)(2,1)S(1)}, bf16[1536,384]{1,0:T(8,128)(2,1)S(1)}, u32[]{:S(2)}, u32[]{:S(2)}) collective-permute-start(bf16[1536,384]{1,0:T(8,128)(2,1)S(1)} %copy-done.7), channel_id=1, source_target_pairs={{0,1},{1,0},{2,3},{3,2},{4,5},{5,4},{6,7},{7,6},{8,9},{9,8},{10,11... | collective-permute-start | bytes 3538952 | tf_op jit(solution)/shard_map/ppermute | solution.py:480
  12.6 21.4 %collective-permute-start.13 = (bf16[384,1536]{1,0:T(8,128)(2,1)S(1)}, bf16[384,1536]{1,0:T(8,128)(2,1)S(1)}, u32[]{:S(2)}, u32[]{:S(2)}) collective-permute-start(bf16[384,1536]{1,0:T(8,128)(2,1)S(1)} %copy-done.6), channel_id=1, source_target_pairs={{0,1},{1,0},{2,3},{3,2},{4,5},{5,4},{6,7},{7,6},{8,9},{9,8},{10,11... | collective-permute-start | bytes 3538952 | tf_op jit(solution)/shard_map/ppermute | solution.py:480
  12.8 11.5 %collective-permute-start.9 = (bf16[512,384]{1,0:T(8,128)(2,1)S(1)}, bf16[512,384]{1,0:T(8,128)(2,1)S(1)}, u32[]{:S(2)}, u32[]{:S(2)}) collective-permute-start(bf16[512,384]{1,0:T(8,128)(2,1)S(1)} %pack.3.refs_0_), channel_id=1, source_target_pairs={{1,2},{2,1},{5,6},{6,5},{9,10},{10,9},{13,14},{14,13},{17,18},{18,... | collective-permute-start | bytes 1179656 | tf_op jit(solution)/shard_map/ppermute | solution.py:573
  19.5 14.4 %collective-permute-start.12 = (bf16[256,768]{1,0:T(8,128)(2,1)S(1)}, bf16[256,768]{1,0:T(8,128)(2,1)S(1)}, u32[]{:S(2)}, u32[]{:S(2)}) collective-permute-start(bf16[256,768]{1,0:T(8,128)(2,1)S(1)} %get-tuple-element.96.refs_0_.refs_6_.refs_4_), channel_id=1, source_target_pairs={{0,2},{2,0},{1,3},{3,1},{4,6},{6,4},{5,7},{7,5},{8,10},{10,8},{9,1... | collective-permute-start | bytes 1179656 | tf_op jit(solution)/shard_map/ppermute | solution.py:476
  25.8 8.1 %collective-permute-start.11 = (bf16[256,384]{1,0:T(8,128)(2,1)S(1)}, bf16[256,384]{1,0:T(8,128)(2,1)S(1)}, u32[]{:S(2)}, u32[]{:S(2)}) collective-permute-start(bf16[256,384]{1,0:T(8,128)(2,1)S(1)} %get-tuple-element.99), channel_id=1, source_target_pairs={{0,1},{1,0},{2,3},{3,2},{4,5},{5,4},{6,7},{7,6},{8,9},{9,8},{10,11... | collective-permute-start | bytes 589832 | tf_op jit(solution)/shard_map/ppermute | solution.py:480
  36.9 6.4 %collective-permute-start.15 = (bf16[256,1920]{1,0:T(8,128)(2,1)S(1)}, bf16[256,1920]{1,0:T(8,128)(2,1)S(1)}, u32[]{:S(2)}, u32[]{:S(2)}) collective-permute-start(bf16[256,1920]{1,0:T(8,128)(2,1)S(1)} %get-tuple-element.110.refs_2_), channel_id=1, source_target_pairs={{0,1},{1,0},{2,3},{3,2},{4,5},{5,4},{6,7},{7,6},{8,9},{9,8},{10,11... | collective-permute-start | bytes 2949128 | tf_op jit(solution)/shard_map/ppermute | solution.py:480
  37.1 3.8 %collective-permute-start.14 = (bf16[256,1536]{1,0:T(8,128)(2,1)S(1)}, bf16[256,1536]{1,0:T(8,128)(2,1)S(1)}, u32[]{:S(2)}, u32[]{:S(2)}) collective-permute-start(bf16[256,1536]{1,0:T(8,128)(2,1)S(1)} %get-tuple-element.104.active.refs_3_), channel_id=1, source_target_pairs={{0,1},{1,0},{2,3},{3,2},{4,5},{5,4},{6,7},{7,6},{8,9},{9,8},{10,11... | collective-permute-start | bytes 2359304 | tf_op jit(solution)/shard_map/ppermute | solution.py:480
  37.5 11.1 %collective-permute-start.16 = (bf16[256,768]{1,0:T(8,128)(2,1)S(1)}, bf16[256,768]{1,0:T(8,128)(2,1)S(1)}, u32[]{:S(2)}, u32[]{:S(2)}) collective-permute-start(bf16[256,768]{1,0:T(8,128)(2,1)S(1)} %get-tuple-element.112.refs_6_), channel_id=1, source_target_pairs={{0,2},{2,0},{1,3},{3,1},{4,6},{6,4},{5,7},{7,5},{8,10},{10,8},{9,1... | collective-permute-start | bytes 1179656 | tf_op jit(solution)/shard_map/ppermute | solution.py:476
  39.5 35.4 %collective-permute-start.24 = (bf16[256,768]{1,0:T(8,128)(2,1)S(1)}, bf16[256,768]{1,0:T(8,128)(2,1)S(1)}, u32[]{:S(2)}, u32[]{:S(2)}) collective-permute-start(bf16[256,768]{1,0:T(8,128)(2,1)S(1)} %get-tuple-element.106.refs_0_.refs_6_), channel_id=1, source_target_pairs={{1,3},{2,0},{5,7},{6,4},{9,11},{10,8},{13,15},{14,12},{17,19},{18,... | collective-permute-start | bytes 1179656 | tf_op jit(solution)/shard_map/ppermute | solution.py:620
  41.8 16.0 %collective-permute-start.17 = (bf16[4,48,1536]{2,1,0:T(8,128)(2,1)S(1)}, bf16[4,48,1536]{2,1,0:T(8,128)(2,1)S(1)}, u32[]{:S(2)}, u32[]{:S(2)}) collective-permute-start(bf16[4,48,1536]{2,1,0:T(8,128)(2,1)S(1)} %get-tuple-element.108.refs_0_), channel_id=1, source_target_pairs={{0,4},{4,0},{8,12},{12,8},{16,20},{20,16},{24,28},{28,24},{1,5},{5... | collective-permute-start | bytes 1769480 | tf_op jit(solution)/shard_map/ppermute | solution.py:488
  44.6 16.2 %collective-permute-start.18 = (bf16[4,192,384]{2,1,0:T(8,128)(2,1)S(1)}, bf16[4,192,384]{2,1,0:T(8,128)(2,1)S(1)}, u32[]{:S(2)}, u32[]{:S(2)}) collective-permute-start(bf16[4,192,384]{2,1,0:T(8,128)(2,1)S(1)} %get-tuple-element.111.refs_0_), channel_id=1, source_target_pairs={{0,8},{4,12},{8,0},{12,4},{16,24},{20,28},{24,16},{28,20},{1,9},{5... | collective-permute-start | bytes 1769480 | tf_op jit(solution)/shard_map/ppermute | solution.py:488
  54.1 8.1 %collective-permute-start.19 = (bf16[1536,256]{1,0:T(8,128)(2,1)S(1)}, bf16[1536,256]{1,0:T(8,128)(2,1)S(1)}, u32[]{:S(2)}, u32[]{:S(2)}) collective-permute-start(bf16[1536,256]{1,0:T(8,128)(2,1)S(1)} %get-tuple-element.121.refs_3_), channel_id=1, source_target_pairs={{0,1},{1,0},{2,3},{3,2},{4,5},{5,4},{6,7},{7,6},{8,9},{9,8},{10,11... | collective-permute-start | bytes 2359304 | tf_op jit(solution)/shard_map/ppermute | solution.py:480
  54.2 12.1 %collective-permute-start.20 = (bf16[272,768]{1,0:T(8,128)(2,1)S(1)}, bf16[272,768]{1,0:T(8,128)(2,1)S(1)}, u32[]{:S(2)}, u32[]{:S(2)}) collective-permute-start(bf16[272,768]{1,0:T(8,128)(2,1)S(1)} %get-tuple-element.115.refs_0_.refs_10_), channel_id=1, source_target_pairs={{0,2},{2,0},{1,3},{3,1},{4,6},{6,4},{5,7},{7,5},{8,10},{10,8},{9,1... | collective-permute-start | bytes 1253384 | tf_op jit(solution)/shard_map/ppermute | solution.py:476
  57.9 16.6 %collective-permute-start.21 = (bf16[2,48,1536]{2,1,0:T(8,128)(2,1)S(1)}, bf16[2,48,1536]{2,1,0:T(8,128)(2,1)S(1)}, u32[]{:S(2)}, u32[]{:S(2)}) collective-permute-start(bf16[2,48,1536]{2,1,0:T(8,128)(2,1)S(1)} %get-tuple-element.126), channel_id=1, source_target_pairs={{0,16},{4,20},{8,24},{12,28},{16,0},{20,4},{24,8},{28,12},{1,17},{... | collective-permute-start | bytes 884744 | tf_op jit(solution)/shard_map/ppermute | solution.py:488
  61.0 13.7 %collective-permute-start.22 = (bf16[2,192,384]{2,1,0:T(8,128)(2,1)S(1)}, bf16[2,192,384]{2,1,0:T(8,128)(2,1)S(1)}, u32[]{:S(2)}, u32[]{:S(2)}) collective-permute-start(bf16[2,192,384]{2,1,0:T(8,128)(2,1)S(1)} %get-tuple-element.128), channel_id=1, source_target_pairs={{0,4},{4,0},{8,12},{12,8},{16,20},{20,16},{24,28},{28,24},{1,5},{5... | collective-permute-start | bytes 884744 | tf_op jit(solution)/shard_map/ppermute | solution.py:488
  63.7 19.1 %collective-permute-start.28 = (bf16[4,48,1536]{2,1,0:T(8,128)(2,1)S(1)}, bf16[4,48,1536]{2,1,0:T(8,128)(2,1)S(1)}, u32[]{:S(2)}, u32[]{:S(2)}) collective-permute-start(bf16[4,48,1536]{2,1,0:T(8,128)(2,1)S(1)} %get-tuple-element.123.refs_0_), channel_id=1, source_target_pairs={{0,4},{4,0},{8,12},{12,8},{16,20},{20,16},{24,28},{28,24},{1,5},{5... | collective-permute-start | bytes 1769480 | tf_op jit(solution)/shard_map/ppermute | solution.py:488
  67.7 7.1 %collective-permute-start.23 = (f32[6,384]{1,0:T(8,128)S(1)}, f32[6,384]{1,0:T(8,128)S(1)}, u32[]{:S(2)}, u32[]{:S(2)}) collective-permute-start(f32[6,384]{1,0:T(8,128)S(1)} %get-tuple-element.130), channel_id=1, source_target_pairs={{0,1},{1,0},{2,3},{3,2},{4,5},{5,4},{6,7},{7,6},{8,9},{9,8},{10,11... | collective-permute-start | bytes 27656 | tf_op jit(solution)/shard_map/ppermute | solution.py:480
  74.8 5.6 %collective-permute-start.27 = (f32[1,24,384]{2,1,0:T(8,128)S(1)}, f32[1,24,384]{2,1,0:T(8,128)S(1)}, u32[]{:S(2)}, u32[]{:S(2)}) collective-permute-start(f32[1,24,384]{2,1,0:T(8,128)S(1)} %payload.1.refs_0_.refs_1_), channel_id=1, source_target_pairs={{0,16},{4,20},{8,24},{12,28},{16,0},{20,4},{24,8},{28,12},{1,17},{... | collective-permute-start | bytes 110600 | tf_op jit(solution)/shard_map/ppermute | solution.py:488
  82.9 13.2 %collective-permute-start.29 = (bf16[2,48,1536]{2,1,0:T(8,128)(2,1)S(1)}, bf16[2,48,1536]{2,1,0:T(8,128)(2,1)S(1)}, u32[]{:S(2)}, u32[]{:S(2)}) collective-permute-start(bf16[2,48,1536]{2,1,0:T(8,128)(2,1)S(1)} %get-tuple-element.144), channel_id=1, source_target_pairs={{0,8},{4,12},{8,0},{12,4},{16,24},{20,28},{24,16},{28,20},{1,9},{5... | collective-permute-start | bytes 884744 | tf_op jit(solution)/shard_map/ppermute | solution.py:488
  84.5 20.9 %collective-permute-start.26 = (f32[256,384]{1,0:T(8,128)S(1)}, f32[256,384]{1,0:T(8,128)S(1)}, u32[]{:S(2)}, u32[]{:S(2)}) collective-permute-start(f32[256,384]{1,0:T(8,128)S(1)} %get-tuple-element.140), channel_id=1, source_target_pairs={{0,1},{1,0},{2,3},{3,2},{4,5},{5,4},{6,7},{7,6},{8,9},{9,8},{10,11... | collective-permute-start | bytes 1179656 | tf_op jit(solution)/shard_map/ppermute | solution.py:480
  84.5 13.0 %collective-permute-start.30 = (f32[2,24,384]{2,1,0:T(8,128)S(1)}, f32[2,24,384]{2,1,0:T(8,128)S(1)}, u32[]{:S(2)}, u32[]{:S(2)}) collective-permute-start(f32[2,24,384]{2,1,0:T(8,128)S(1)} %join.3.refs_0_.refs_1_), channel_id=1, source_target_pairs={{0,8},{4,12},{8,0},{12,4},{16,24},{20,28},{24,16},{28,20},{1,9},{5... | collective-permute-start | bytes 221192 | tf_op jit(solution)/shard_map/ppermute | solution.py:488
  85.0 14.1 %collective-permute-start.31 = (bf16[1,48,1536]{2,1,0:T(8,128)(2,1)S(1)}, bf16[1,48,1536]{2,1,0:T(8,128)(2,1)S(1)}, u32[]{:S(2)}, u32[]{:S(2)}) collective-permute-start(bf16[1,48,1536]{2,1,0:T(8,128)(2,1)S(1)} %get-tuple-element.146), channel_id=1, source_target_pairs={{0,8},{4,12},{8,0},{12,4},{16,24},{20,28},{24,16},{28,20},{1,9},{5... | collective-permute-start | bytes 442376 | tf_op jit(solution)/shard_map/ppermute | solution.py:488
  86.6 15.0 %collective-permute-start.32 = (bf16[1,192,384]{2,1,0:T(8,128)(2,1)S(1)}, bf16[1,192,384]{2,1,0:T(8,128)(2,1)S(1)}, u32[]{:S(2)}, u32[]{:S(2)}) collective-permute-start(bf16[1,192,384]{2,1,0:T(8,128)(2,1)S(1)} %get-tuple-element.148), channel_id=1, source_target_pairs={{0,16},{4,20},{8,24},{12,28},{16,0},{20,4},{24,8},{28,12},{1,17},{... | collective-permute-start | bytes 442376 | tf_op jit(solution)/shard_map/ppermute | solution.py:488
  96.1 9.4 %collective-permute-start.25 = (bf16[256,384]{1,0:T(8,128)(2,1)S(1)}, bf16[256,384]{1,0:T(8,128)(2,1)S(1)}, u32[]{:S(2)}, u32[]{:S(2)}) collective-permute-start(bf16[256,384]{1,0:T(8,128)(2,1)S(1)} %get-tuple-element.137), channel_id=1, source_target_pairs={{0,1},{1,0},{2,3},{3,2},{4,5},{5,4},{6,7},{7,6},{8,9},{9,8},{10,11... | collective-permute-start | bytes 589832 | tf_op jit(solution)/shard_map/ppermute | solution.py:480
  97.5 5.2 %collective-permute-start.33 = (f32[4,24,384]{2,1,0:T(8,128)S(1)}, f32[4,24,384]{2,1,0:T(8,128)S(1)}, u32[]{:S(2)}, u32[]{:S(2)}) collective-permute-start(f32[4,24,384]{2,1,0:T(8,128)S(1)} %join.4.refs_0_.refs_1_), channel_id=1, source_target_pairs={{0,4},{4,0},{8,12},{12,8},{16,20},{20,16},{24,28},{28,24},{1,5},{5... | collective-permute-start | bytes 442376 | tf_op jit(solution)/shard_map/ppermute | solution.py:488
  99.1 8.4 %collective-permute-start.35 = (bf16[1,48,1536]{2,1,0:T(8,128)(2,1)S(1)}, bf16[1,48,1536]{2,1,0:T(8,128)(2,1)S(1)}, u32[]{:S(2)}, u32[]{:S(2)}) collective-permute-start(bf16[1,48,1536]{2,1,0:T(8,128)(2,1)S(1)} %get-tuple-element.158), channel_id=1, source_target_pairs={{0,16},{4,20},{8,24},{12,28},{16,0},{20,4},{24,8},{28,12},{1,17},{... | collective-permute-start | bytes 442376 | tf_op jit(solution)/shard_map/ppermute | solution.py:488
  (18 other events, 50.7 us)
where the time goes:
time: 109 us; the launch traced here: 108 us
  waiting for transfers between devices  40.4 us (37%)
  starting transfers between devices  34.9 us (32%)
  Pallas kernels  28 us (26%)
  local copies, waits for them, and re-layouts  2.47 us (2%)
    pallas_call x31, Pallas kernels, call(): pl.pallas_call(body if count else kernel, out_shape=[jax.ShapeDtypeStruct...  28 us
    ppermute x12, waiting for transfers between devices, swap_bit(): lax.ppermute(values, 'dp', [(p, p ^ 1 << bit) for p in range(dp_size)])  25.3 us
    ppermute x12, starting transfers between devices, swap_bit(): lax.ppermute(values, 'dp', [(p, p ^ 1 << bit) for p in range(dp_size)])  17.3 us
    ppermute x4, waiting for transfers between devices, row_swap(): return lax.ppermute(values, 'row', SWAP)  13 us
    ppermute x4, starting transfers between devices, row_swap(): return lax.ppermute(values, 'row', SWAP)  10.6 us
    ppermute x17, starting transfers between devices, col_swap(): return lax.ppermute(values, 'col', SWAP)  4.06 us
    unnamed x29, local copies, waits for them, and re-layouts  2.47 us
  transfers between devices with their start and end apart: 36, of which 16 were waited for; matrix products, arithmetic and copies ran while one was open for 2% of the time, Pallas kernels for 22%

commit v1 on v0

--- a/solution.py
+++ b/solution.py
@@ -119,7 +119,7 @@
 
 def first_kernel(
     normal, keep, other, other_col, qkv_own, qkv_peer, out_own, out_peer,
-    mod, bias, normed_own, normed_peer, packed, attended, part,
+    mod, bias, normed_own, normed_peer, packed, attended, part, probs_all,
 ):
     mods = halves(keep[...], other_col[0:6, :])
     mod[...] = mods
@@ -149,8 +149,9 @@
         query, key, value = full[0:64], full[64:128], full[128:192]
         scores = mm(key, query, (0, 0)) * 0.125
         expon = jnp.exp(scores - jnp.max(scores, axis=0, keepdims=True))
-        probs = (expon * (1.0 / jnp.sum(expon, axis=0, keepdims=True))).astype(BF16)
-        attended[h * 64 : h * 64 + 64, :] = mm(value, probs, (1, 0)).astype(BF16)
+        probs = expon * (1.0 / jnp.sum(expon, axis=0, keepdims=True))
+        probs_all[h] = probs
+        attended[h * 64 : h * 64 + 64, :] = mm(value, probs.astype(BF16), (1, 0)).astype(BF16)
     part[:, :HALF] = mm(attended[...], out_own[...], (0, 0)).astype(BF16)
     part[:, HALF:] = mm(attended[...], out_peer[...], (0, 0)).astype(BF16)
 
@@ -181,12 +182,14 @@
 
 def second_kernel(
     lat, mod, bias, part, part_recv, up_own, up_peer, up_bias, grad_active,
-    normed_own, active, hidden, part_two,
+    normed_own, active, hidden, part_two, normal_two, inverse_two,
 ):
     shift, scale = mod[3:4, :], 1.0 + mod[4:5, :]
     for rows in blocks():
         resid, unused = resid_of(lat, mod, bias, part, part_recv, rows)
-        normal, unused = norm_of(resid)
+        normal, inverse = norm_of(resid)
+        normal_two[rows, :] = normal
+        inverse_two[rows, :] = jnp.broadcast_to(inverse, (inverse.shape[0], 128))
         normed = (normal * scale + shift).astype(BF16)
         normed_own[rows, :] = normed[:, :HALF]
         hidden[rows, FEED:] = normed[:, HALF:]
@@ -253,14 +256,13 @@
 
 
 def third_kernel(
-    lat, mod, bias, part, part_recv, grad_two, grad_two_recv, cot, packed, sums,
+    normal_two, inverse_two, probs_all, mod, grad_two, grad_two_recv, cot, packed, sums,
     qkv_own, qkv_peer, out_own, out_peer,
     grad_resid, grad_own, grad_packed, part_three, grad_peer,
 ):
     gate, scale = mod[2:3, :], 1.0 + mod[4:5, :]
     for rows in blocks():
-        resid, unused = resid_of(lat, mod, bias, part, part_recv, rows)
-        normal, inverse = norm_of(resid)
+        normal, inverse = normal_two[rows, :], inverse_two[rows, 0:1]
         weighted = (grad_two[rows, :].astype(F32) + grad_two_recv[rows, :].astype(F32)) * scale
         back = inverse * (weighted - row_mean(weighted) - normal * row_mean(weighted * normal))
         grads = cot[rows, :].astype(F32) + back
@@ -275,9 +277,7 @@
         wide = slice(h * 64, h * 64 + 64)
         grad_att = mm(out_own[wide, :], grad_own[...], (1, 1)) + mm(out_peer[wide, :], grad_peer[...], (1, 1))
         grad_att = grad_att.astype(BF16)
-        scores = mm(key, query, (0, 0)) * 0.125
-        expon = jnp.exp(scores - jnp.max(scores, axis=0, keepdims=True))
-        probs = expon * (1.0 / jnp.sum(expon, axis=0, keepdims=True))
+        probs = probs_all[h]
         grad_probs = mm(value, grad_att, (0, 0))
         total = jnp.sum(probs * grad_probs, axis=0, keepdims=True)
         grad_scores = (probs * (grad_probs - total)).astype(BF16)
@@ -313,14 +313,13 @@
 
 def last_kernel(
     lat, mod, bias, part, part_recv, grad_two, grad_two_recv, cot,
-    grad_resid, grad_one, grad_one_recv, branch_sums,
+    grad_resid, grad_one, grad_one_recv, branch_sums, normal_two,
     lat_own, lat_peer, mod_own, mod_peer,
 ):
     scale = 1.0 + mod[1:2, :]
     sums = [jnp.zeros((1, D), F32)] * 6
     for rows in blocks():
-        resid, one = resid_of(lat, mod, bias, part, part_recv, rows)
-        normal_two, unused = norm_of(resid)
+        one = branch(part, part_recv, bias[0:1, :], rows)
         normal, inverse = norm_of(lat[rows, :].astype(F32))
         normed_grad = grad_one[rows, :].astype(F32) + grad_one_recv[rows, :].astype(F32)
         normed_two = grad_two[rows, :].astype(F32) + grad_two_recv[rows, :].astype(F32)
@@ -335,7 +334,7 @@
             normed_grad * normal,
             resid_grad * one,
             normed_two,
-            normed_two * normal_two,
+            normed_two * normal_two[rows, :],
             cot[rows, :].astype(F32),
         )
         sums = [s + jnp.sum(t, axis=0, keepdims=True) for s, t in zip(sums, terms)]
@@ -541,8 +540,8 @@
     rows_down, rows_up = HALF // dp_size, FEED // dp_size
     every = tuple(range(bits))
     left = every[::-1]
-    up = Sums("up_add", every[1:2] + every[:1] + every[2:], dp_size)
-    down = Sums("down_add", every[:1] + every[2:] + every[1:2], dp_size)
+    up = Sums("up_add", every[1:] + every[:1], dp_size)
+    down = Sums("down_add", every, dp_size)
     proj = Sums("proj_add", every, dp_size)
     change = [(1, 2), (2, 1)]
     classes = class_table.shape[0]
@@ -585,9 +584,9 @@
     )
     up_weight, down_weight = lax.optimization_barrier((up_weight, down_weight, other_col))[:2]
     down_peer, up_peer = col_swap(down_weight), col_swap(up_weight)
-    mod, bias, normed_own, normed_peer, packed, attended, part_one = call(
+    mod, bias, normed_own, normed_peer, packed, attended, part_one, probs_all = call(
         first_kernel,
-        [((6, D), F32), ((8, D), F32), (slim, BF16), (slim, BF16), ((QKV, SEQ), BF16), ((HALF, SEQ), BF16), (wide, BF16)],
+        [((6, D), F32), ((8, D), F32), (slim, BF16), (slim, BF16), ((QKV, SEQ), BF16), ((HALF, SEQ), BF16), (wide, BF16), ((HEADS, SEQ, SEQ), F32)],
         [normal, keep, other, other_col, qkv_own, qkv_peer, out_own, out_peer],
         5,
         "first",
@@ -604,9 +603,9 @@
     normed_recv, attended_recv = col_swap(normed_peer), col_swap(attended)
     two_grad_recv = col_swap(two_grad_peer)
     resid_args = [lat, mod, bias, part_one, part_one_recv]
-    second_own, active, hidden, part_two = call(
+    second_own, active, hidden, part_two, normal_two, inverse_two = call(
         second_kernel,
-        [(slim, BF16), ((SEQ, FEED), BF16), ((SEQ, FEED + HALF), BF16), (wide, BF16)],
+        [(slim, BF16), ((SEQ, FEED), BF16), ((SEQ, FEED + HALF), BF16), (wide, BF16), (wide, F32), ((SEQ, 128), F32)],
         [*resid_args, up_weight, up_peer, up_bias, grad_active],
         4,
         "second",
@@ -617,7 +616,6 @@
     branch_part, branch_sums = call(
         down_kernel, [(wide, BF16), ((8, D), F32)], [active, cot, down_weight, down_peer], 1, "down"
     )
-    branch_recv = lax.ppermute(branch_part, ("row", "col"), [(1, 3), (2, 0)])
     down_send, down_keep, down_sum = call(
         functools.partial(down_grad_kernel, left, down.order[0]),
         [((pieces, rows_down, FEED), BF16), ((pieces, rows_down, FEED), BF16), ((1, HALF), F32)],
@@ -639,15 +637,18 @@
     grad_resid, one_grad_own, grad_packed, part_three = call(
         third_kernel,
         [(wide, F32), (slim, BF16), ((QKV + HALF, SEQ), BF16), ((SEQ + 16, D), BF16)],
-        [*resid_args, part_two, part_two_recv, cot, packed, branch_sums, qkv_own, qkv_peer, out_own, out_peer],
+        [normal_two, inverse_two, probs_all, mod, part_two, part_two_recv, cot, packed, branch_sums, qkv_own, qkv_peer, out_own, out_peer],
         20,
         "third",
         [up_send],
         [pltpu.VMEM(slim, BF16)],
     )
     part_three_recv = row_swap(part_three)
+    branch_recv = lax.ppermute(
+        lax.optimization_barrier((branch_part, part_three))[0], ("row", "col"), [(1, 3), (2, 0)]
+    )
     packed_recv = col_swap(grad_packed)
-    token = down.advance([part_three], 6)
+    token = down.advance([part_three], 0.3)
     token = up.advance([token], 6)
     proj_send, proj_keep, out_sum, pack_sum = call(
         functools.partial(proj_grad_kernel, left, proj.order[0]),
@@ -667,14 +668,13 @@
     lat_grad_own, lat_grad_peer, mod_own, mod_peer = call(
         last_kernel,
         [(slim, F32), (slim, F32), ((6, HALF), F32), ((6, HALF), F32)],
-        [*resid_args, part_two, part_two_recv, cot, grad_resid, part_three, part_three_recv, branch_sums],
+        [*resid_args, part_two, part_two_recv, cot, grad_resid, part_three, part_three_recv, branch_sums, normal_two],
         20,
         "last",
         [token],
     )
     mod_recv = col_swap(mod_peer)
-    token = down.advance([mod_own])
-    token = up.advance([token], 3)
+    token = down.advance([mod_own], 3.3)
     (payload,) = call(
         payload_kernel,
         [((1, 24, HALF), F32)],
@@ -698,18 +698,18 @@
     for step, bit in enumerate(every[::-1]):
         recv = swap_bit(payload, bit, dp_size)
         if step == 1:
-            token = proj.advance([token], 20)
-            while min(down.step, up.step) + 1 < bits:
-                for part in (down, up):
-                    token = part.advance([token], 0.1)
+            token = up.advance([token], 0.1)
+            token = proj.advance([token], 0.1)
             token = proj.advance([token], 0.1)
         if step == 2:
+            while down.step + 1 < bits:
+                token = down.advance([token], 0.1)
             down_grad, token = down.finish(sum_kernel, [((rows_down, FEED), F32), mark], [token], 0.1)
-            up_grad, token = up.finish(sum_kernel, [((rows_up, HALF), F32), mark], [token], 0.1)
         (payload,) = call(join_kernel, [((2 << step, 24, HALF), F32)], [payload, recv], 0.1, "join", [token])
         token = payload
-    while proj.step + 1 < bits:
-        token = proj.advance([token])
+    while min(up.step, proj.step) + 1 < bits:
+        for part in (up, proj):
+            token = part.advance([token], 0.1)
     width = HALF // dp_size
     mod_grad, mod_bias_grad, up_bias_grad, down_bias_grad, out_bias_grad, pack_grad, mod_mark = call(
         mod_sum_kernel,
@@ -737,10 +737,11 @@
         0.5,
         "finish",
     )
+    up_grad, token = up.finish(sum_kernel, [((rows_up, HALF), F32), mark], [finish_mark], 0.1)
     qkv_grad, out_grad = proj.finish(
         proj_sum_kernel,
         [((3 * HEADS, rows_down, HD), F32), ((HEADS, rows_down, HD), F32)],
-        [finish_mark],
+        [token],
     )
     return (
         output,

time: 109 us -> 102 us (0.936)
  starting transfers between devices: 34.9 us -> 30.3 us
  Pallas kernels: 28 us -> 26.8 us
  waiting for transfers between devices: 40.4 us -> 39.2 us
    ppermute x12, starting transfers between devices: 17.3 us -> 13.8 us  [swap_bit(): lax.ppermute(values, 'dp', [(p, p ^ 1 << bit) for p in range(dp_size)])]
    ppermute x12, waiting for transfers between devices: 25.3 us -> 23.7 us  [swap_bit(): lax.ppermute(values, 'dp', [(p, p ^ 1 << bit) for p in range(dp_size)])]
    ppermute x17, waiting for transfers between devices: 2.12 us -> 3.37 us  [col_swap(): return lax.ppermute(values, 'col', SWAP)]
    pallas_call x31, Pallas kernels: 28 us -> 26.8 us  [call(): pl.pallas_call(body if count else kernel, out_shape=[jax.ShapeDtypeStruct...]
where the time goes in v1:
time: 102 us
  waiting for transfers between devices  39.2 us (38%)
  starting transfers between devices  30.3 us (30%)
  Pallas kernels  26.8 us (26%)
  local copies, waits for them, and re-layouts  2.43 us (2%)
    pallas_call x31, Pallas kernels, call(): pl.pallas_call(body if count else kernel, out_shape=[jax.ShapeDtypeStruct...  26.8 us
    ppermute x12, waiting for transfers between devices, swap_bit(): lax.ppermute(values, 'dp', [(p, p ^ 1 << bit) for p in range(dp_size)])  23.7 us
    ppermute x12, starting transfers between devices, swap_bit(): lax.ppermute(values, 'dp', [(p, p ^ 1 << bit) for p in range(dp_size)])  13.8 us
    ppermute x4, waiting for transfers between devices, row_swap(): return lax.ppermute(values, 'row', SWAP)  12.1 us
    ppermute x4, starting transfers between devices, row_swap(): return lax.ppermute(values, 'row', SWAP)  9.66 us
    ppermute x17, starting transfers between devices, col_swap(): return lax.ppermute(values, 'col', SWAP)  4.13 us
    ppermute x17, waiting for transfers between devices, col_swap(): return lax.ppermute(values, 'col', SWAP)  3.37 us
    unnamed x29, local copies, waits for them, and re-layouts  2.43 us
  transfers between devices with their start and end apart: 36, of which 16 were waited for; matrix products, arithmetic and copies ran while one was open for 2% of the time, Pallas kernels for 22%

profile of v1, /device:TPU:0, one launch (start us, length us, event | category | flops | bytes accessed | tf_op | source)
XLA Modules:
  0.0 101.5 jit_solution(16640598679491162646)
XLA Ops:
  3.5 1.5 %copy-done.1 = bf16[384,6,384]{2,0,1:T(8,128)(2,1)S(1)} copy-done((bf16[384,6,384]{2,0,1:T(8,128)(2,1)S(1)}, bf16[384,6,384]{2,0,1:T(8,128)(2,1)}, u32[]{:S(2)}) %copy-start.1) | copy-done | bytes 1769496
  5.4 3.0 %collective-permute-start.4 = (f32[16,384]{1,0:T(8,128)S(1)}, f32[16,384]{1,0:T(8,128)S(1)}, u32[]{:S(2)}, u32[]{:S(2)}) collective-permute-start(f32[16,384]{1,0:T(8,128)S(1)} %get-tuple-element.94.refs_0_.refs_3_), channel_id=1, source_target_pairs={{0,2},{2,0},{1,3},{3,1},{4,6},{6,4},{5,7},{7,5},{8,10},{10,8},{9,1... | collective-permute-start | bytes 73736 | tf_op jit(solution)/shard_map/ppermute | solution.py:475
  10.3 1.1 %collective-permute-start.6 = (f32[16,384]{1,0:T(8,128)S(1)}, f32[16,384]{1,0:T(8,128)S(1)}, u32[]{:S(2)}, u32[]{:S(2)}) collective-permute-start(f32[16,384]{1,0:T(8,128)S(1)} %get-tuple-element.97.other), channel_id=1, source_target_pairs={{0,1},{1,0},{2,3},{3,2},{4,5},{5,4},{6,7},{7,6},{8,9},{9,8},{10,11... | collective-permute-start | bytes 73736 | tf_op jit(solution)/shard_map/ppermute | solution.py:479
  14.7 4.8 %first.1 = (f32[6,768]{1,0:T(8,128)S(1)}, f32[8,768]{1,0:T(8,128)S(1)}, bf16[256,384]{1,0:T(8,128)(2,1)S(1)}, bf16[256,384]{1,0:T(8,128)(2,1)S(1)}, bf16[1152,25...) custom-call(f32[256,768]{1,0:T(8,128)S(1)} %get-tuple-element.96.nor, ...), custom_call_target="tpu_custom_call" | custom-call | flops 5750000128 | bytes 1024 | tf_op jit(solution)/shard_map/first/pallas_call | solution.py:39
  19.5 4.8 %collective-permute-start.12 = (bf16[256,768]{1,0:T(8,128)(2,1)S(1)}, bf16[256,768]{1,0:T(8,128)(2,1)S(1)}, u32[]{:S(2)}, u32[]{:S(2)}) collective-permute-start(bf16[256,768]{1,0:T(8,128)(2,1)S(1)} %get-tuple-element.100.refs_0_.refs_6_.refs_4_), channel_id=1, source_target_pairs={{0,2},{2,0},{1,3},{3,1},{4,6},{6,4},{5,7},{7,5},{8,10},{10,8},{9,1... | collective-permute-start | bytes 1179656 | tf_op jit(solution)/shard_map/ppermute | solution.py:475
  24.8 1.0 %early.1 = (bf16[256,768]{1,0:T(8,128)(2,1)S(1)}, bf16[256,384]{1,0:T(8,128)(2,1)S(1)}, bf16[256,384]{1,0:T(8,128)(2,1)S(1)}, f32[256,1536]{1,0:T(8,128)S(1)}) custom-call(bf16[256,768]{1,0:T(8,128)(2,1)S(1)} %get-tuple-element.100.refs_0_.refs_6_.refs_4_, bf16[256,384]{1,0:T(8,128)(2,1)S(1)} %copy-done.11, ...), custom_call_target="tpu_custom_call" | custom-call | flops 1150000000 | bytes 1024 | tf_op jit(solution)/shard_map/early/pallas_call | solution.py:39
  26.0 8.0 %collective-permute-done.12.refs_7_.refs_5_ = bf16[256,768]{1,0:T(8,128)(2,1)S(1)} collective-permute-done((bf16[256,768]{1,0:T(8,128)(2,1)S(1)}, bf16[256,768]{1,0:T(8,128)(2,1)S(1)}, u32[]{:S(2)}, u32[]{:S(2)}) %collective-permute-start.12) | collective-permute-done | bytes 393248 | tf_op jit(solution)/shard_map/ppermute | solution.py:475
  34.0 3.0 %second.1 = (bf16[256,384]{1,0:T(8,128)(2,1)S(1)}, bf16[256,1536]{1,0:T(8,128)(2,1)S(1)}, bf16[256,1920]{1,0:T(8,128)(2,1)S(1)}, bf16[256,768]{1,0:T(8,128)(2,1)...) custom-call(bf16[256,384]{1,0:T(8,128)(2,1)S(1)} %collective-permute-done.7.refs_0_.refs_2_, ...), custom_call_target="tpu_custom_call" | custom-call | flops 4600000000 | bytes 1024 | tf_op jit(solution)/shard_map/second/pallas_call | solution.py:39
  38.4 1.0 down.1
  39.4 1.3 %collective-permute-done.14.refs_4_ = bf16[256,1536]{1,0:T(8,128)(2,1)S(1)} collective-permute-done((bf16[256,1536]{1,0:T(8,128)(2,1)S(1)}, bf16[256,1536]{1,0:T(8,128)(2,1)S(1)}, u32[]{:S(2)}, u32[]{:S(2)}) %collective-permute-start.14) | collective-permute-done | bytes 786464 | tf_op jit(solution)/shard_map/ppermute | solution.py:479
  41.5 1.5 %collective-permute-start.17 = (bf16[4,48,1536]{2,1,0:T(8,128)(2,1)S(1)}, bf16[4,48,1536]{2,1,0:T(8,128)(2,1)S(1)}, u32[]{:S(2)}, u32[]{:S(2)}) collective-permute-start(bf16[4,48,1536]{2,1,0:T(8,128)(2,1)S(1)} %get-tuple-element.112.refs_0_), channel_id=1, source_target_pairs={{0,4},{4,0},{8,12},{12,8},{16,20},{20,16},{24,28},{28,24},{1,5},{5... | collective-permute-start | bytes 1769480 | tf_op jit(solution)/shard_map/ppermute | solution.py:487
  43.0 1.2 %up_grad.1 = (bf16[4,192,384]{2,1,0:T(8,128)(2,1)S(1)}, bf16[4,192,384]{2,1,0:T(8,128)(2,1)S(1)}, f32[1,1536]{1,0:T(1,128)S(1)}) custom-call(bf16[4,48,1536]{2,1,0:T(8,128)(2,1)S(1)} %get-tuple-element.112.refs_0_, bf16[256,384]{1,0:T(8,128)(2,1)S(1)} %get-tuple-element.113.refs_1_, bf16[256,1920]{1,0:T(8,128)(2,1)S(1)} %get-tuple-element.114.refs_2_, ...), custom_call_target="tpu_custom_call" | custom-call | flops 1380000000 | bytes 1024 | tf_op jit(solution)/shard_map/up_grad/pallas_call | solution.py:39
  44.3 1.6 %collective-permute-start.18 = (bf16[4,192,384]{2,1,0:T(8,128)(2,1)S(1)}, bf16[4,192,384]{2,1,0:T(8,128)(2,1)S(1)}, u32[]{:S(2)}, u32[]{:S(2)}) collective-permute-start(bf16[4,192,384]{2,1,0:T(8,128)(2,1)S(1)} %get-tuple-element.115.refs_0_), channel_id=1, source_target_pairs={{0,8},{4,12},{8,0},{12,4},{16,24},{20,28},{24,16},{28,20},{1,9},{5... | collective-permute-start | bytes 1769480 | tf_op jit(solution)/shard_map/ppermute | solution.py:487
  45.9 2.7 %collective-permute-done.16.refs_6_.refs_7_ = bf16[256,768]{1,0:T(8,128)(2,1)S(1)} collective-permute-done((bf16[256,768]{1,0:T(8,128)(2,1)S(1)}, bf16[256,768]{1,0:T(8,128)(2,1)S(1)}, u32[]{:S(2)}, u32[]{:S(2)}) %collective-permute-start.16) | collective-permute-done | bytes 393248 | tf_op jit(solution)/shard_map/ppermute | solution.py:475
  48.6 4.4 %third.1 = (f32[256,768]{1,0:T(8,128)S(1)}, bf16[256,384]{1,0:T(8,128)(2,1)S(1)}, bf16[1536,256]{1,0:T(8,128)(2,1)S(1)}, bf16[272,768]{1,0:T(8,128)(2,1)S(1)}) custom-call(bf16[4,192,384]{2,1,0:T(8,128)(2,1)S(1)} %get-tuple-element.115.refs_0_, f32[256,768]{1,0:T(8,128)S(1)} %get-tuple-element.116.refs_1_.refs_13_, ...), custom_call_target="tpu_custom_call" | custom-call | flops 23000000512 | bytes 1024 | tf_op jit(solution)/shard_map/third/pallas_call | solution.py:39
  53.1 1.0 collective-permute-start.20
  54.1 1.3 %collective-permute-start.23 = (bf16[256,768]{1,0:T(8,128)(2,1)S(1)}, bf16[256,768]{1,0:T(8,128)(2,1)S(1)}, u32[]{:S(2)}, u32[]{:S(2)}) collective-permute-start(bf16[256,768]{1,0:T(8,128)(2,1)S(1)} %get-tuple-element.141.refs_0_.refs_6_), channel_id=1, source_target_pairs={{1,3},{2,0},{5,7},{6,4},{9,11},{10,8},{13,15},{14,12},{17,19},{18,... | collective-permute-start | bytes 1179656 | tf_op jit(solution)/shard_map/ppermute | solution.py:647
  55.4 1.6 %collective-permute-done.17.refs_2_ = bf16[4,48,1536]{2,1,0:T(8,128)(2,1)S(1)} collective-permute-done((bf16[4,48,1536]{2,1,0:T(8,128)(2,1)S(1)}, bf16[4,48,1536]{2,1,0:T(8,128)(2,1)S(1)}, u32[]{:S(2)}, u32[]{:S(2)}) %collective-permute-start.17) | collective-permute-done | bytes 589856 | tf_op jit(solution)/shard_map/ppermute | solution.py:487
  57.1 1.6 %collective-permute-start.21 = (bf16[2,48,1536]{2,1,0:T(8,128)(2,1)S(1)}, bf16[2,48,1536]{2,1,0:T(8,128)(2,1)S(1)}, u32[]{:S(2)}, u32[]{:S(2)}) collective-permute-start(bf16[2,48,1536]{2,1,0:T(8,128)(2,1)S(1)} %get-tuple-element.133), channel_id=1, source_target_pairs={{0,8},{4,12},{8,0},{12,4},{16,24},{20,28},{24,16},{28,20},{1,9},{5... | collective-permute-start | bytes 884744 | tf_op jit(solution)/shard_map/ppermute | solution.py:487
  59.6 2.6 %collective-permute-start.27 = (bf16[2,192,384]{2,1,0:T(8,128)(2,1)S(1)}, bf16[2,192,384]{2,1,0:T(8,128)(2,1)S(1)}, u32[]{:S(2)}, u32[]{:S(2)}) collective-permute-start(bf16[2,192,384]{2,1,0:T(8,128)(2,1)S(1)} %get-tuple-element.148), channel_id=1, source_target_pairs={{0,16},{4,20},{8,24},{12,28},{16,0},{20,4},{24,8},{28,12},{1,17},{... | collective-permute-start | bytes 884744 | tf_op jit(solution)/shard_map/ppermute | solution.py:487
  62.3 1.4 %proj_grad.1 = (bf16[4,48,1536]{2,1,0:T(8,128)(2,1)S(1)}, bf16[4,48,1536]{2,1,0:T(8,128)(2,1)S(1)}, f32[1,384]{1,0:T(1,128)S(1)}, f32[1,576]{1,0:T(1,128)S(1)}) custom-call(bf16[2,192,384]{2,1,0:T(8,128)(2,1)S(1)} %get-tuple-element.126.refs_0_.refs_1_, bf16[256,384]{1,0:T(8,128)(2,1)S(1)} %get-tuple-element.127.refs_1_, ...), custom_call_target="tpu_custom_call" | custom-call | flops 1495000064 | bytes 1024 | tf_op jit(solution)/shard_map/proj_grad/pallas_call | solution.py:39
  65.2 1.2 %last.1 = (f32[256,384]{1,0:T(8,128)S(1)}, f32[256,384]{1,0:T(8,128)S(1)}, f32[6,384]{1,0:T(8,128)S(1)}, f32[6,384]{1,0:T(8,128)S(1)}) custom-call(bf16[4,48,1536]{2,1,0:T(8,128)(2,1)S(1)} %get-tuple-element.130.refs_0_, bf16[256,768]{1,0:T(8,128)(2,1)S(1)} %get-tuple-element.104.refs_3_.refs_1_, f32[6,768]{1,0:T(8,128)S(1)} %get-tuple-element.101.refs_4_.refs_2_, ...), custom_call_target="tpu_custom_call" | custom-call | flops 23000000512 | bytes 1024 | tf_op jit(solution)/shard_map/last/pallas_call | solution.py:39
  66.5 5.7 %collective-permute-done.21.refs_2_ = bf16[2,48,1536]{2,1,0:T(8,128)(2,1)S(1)} collective-permute-done((bf16[2,48,1536]{2,1,0:T(8,128)(2,1)S(1)}, bf16[2,48,1536]{2,1,0:T(8,128)(2,1)S(1)}, u32[]{:S(2)}, u32[]{:S(2)}) %collective-permute-start.21) | collective-permute-done | bytes 294944 | tf_op jit(solution)/shard_map/ppermute | solution.py:487
  72.8 4.5 %collective-permute-done.26.refs_2_ = f32[1,24,384]{2,1,0:T(8,128)S(1)} collective-permute-done((f32[1,24,384]{2,1,0:T(8,128)S(1)}, f32[1,24,384]{2,1,0:T(8,128)S(1)}, u32[]{:S(2)}, u32[]{:S(2)}) %collective-permute-start.26) | collective-permute-done | bytes 36896 | tf_op jit(solution)/shard_map/ppermute | solution.py:487
  78.0 1.5 %collective-permute-start.29 = (bf16[2,48,1536]{2,1,0:T(8,128)(2,1)S(1)}, bf16[2,48,1536]{2,1,0:T(8,128)(2,1)S(1)}, u32[]{:S(2)}, u32[]{:S(2)}) collective-permute-start(bf16[2,48,1536]{2,1,0:T(8,128)(2,1)S(1)} %get-tuple-element.152), channel_id=1, source_target_pairs={{0,8},{4,12},{8,0},{12,4},{16,24},{20,28},{24,16},{28,20},{1,9},{5... | collective-permute-start | bytes 884744 | tf_op jit(solution)/shard_map/ppermute | solution.py:487
  80.1 1.0 %collective-permute-start.31 = (bf16[1,48,1536]{2,1,0:T(8,128)(2,1)S(1)}, bf16[1,48,1536]{2,1,0:T(8,128)(2,1)S(1)}, u32[]{:S(2)}, u32[]{:S(2)}) collective-permute-start(bf16[1,48,1536]{2,1,0:T(8,128)(2,1)S(1)} %get-tuple-element.154), channel_id=1, source_target_pairs={{0,16},{4,20},{8,24},{12,28},{16,0},{20,4},{24,8},{28,12},{1,17},{... | collective-permute-start | bytes 442376 | tf_op jit(solution)/shard_map/ppermute | solution.py:487
  81.2 7.8 %collective-permute-done.29.refs_2_ = bf16[2,48,1536]{2,1,0:T(8,128)(2,1)S(1)} collective-permute-done((bf16[2,48,1536]{2,1,0:T(8,128)(2,1)S(1)}, bf16[2,48,1536]{2,1,0:T(8,128)(2,1)S(1)}, u32[]{:S(2)}, u32[]{:S(2)}) %collective-permute-start.29) | collective-permute-done | bytes 294944 | tf_op jit(solution)/shard_map/ppermute | solution.py:487
  89.8 2.2 %collective-permute-start.32 = (f32[4,24,384]{2,1,0:T(8,128)S(1)}, f32[4,24,384]{2,1,0:T(8,128)S(1)}, u32[]{:S(2)}, u32[]{:S(2)}) collective-permute-start(f32[4,24,384]{2,1,0:T(8,128)S(1)} %join.4.refs_0_.refs_1_), channel_id=1, source_target_pairs={{0,4},{4,0},{8,12},{12,8},{16,20},{20,16},{24,28},{28,24},{1,5},{5... | collective-permute-start | bytes 442376 | tf_op jit(solution)/shard_map/ppermute | solution.py:487
  92.8 2.3 %collective-permute-done.32.refs_2_ = f32[4,24,384]{2,1,0:T(8,128)S(1)} collective-permute-done((f32[4,24,384]{2,1,0:T(8,128)S(1)}, f32[4,24,384]{2,1,0:T(8,128)S(1)}, u32[]{:S(2)}, u32[]{:S(2)}) %collective-permute-start.32) | collective-permute-done | bytes 147488 | tf_op jit(solution)/shard_map/ppermute | solution.py:487
  95.1 1.9 %mod_sum.1 = (f32[6,48,384]{2,1,0:T(8,128)}, f32[6,1,48]{2,1,0:T(1,128)}, f32[1,192]{1,0:T(1,128)}, f32[1,48]{1,0:T(1,128)}, f32[1,48]{1,0:T(1,128)}, /*index=5*/f32[3,2,8]{2,1,0:T(2,128)}, f32[8,128]{1,0:T(8,128)S(1)}) custom-call(f32[8,24,384]{2,1,0:T(8,128)S(1)} %join.5.refs_0_.refs_1_, f32[8,24,384]{2,1,0:T(8,128)S(1)} %join.5.refs_0_.refs_1_), custom_call_target="tpu_custom_call" | custom-call | flops 115000000 | bytes 1024 | tf_op jit(solution)/shard_map/mod_sum/pallas_call | solution.py:39
  97.8 1.2 %collective-permute-done.33.part_recv = f32[2,384]{1,0:T(2,128)S(1)} collective-permute-done((f32[2,384]{1,0:T(2,128)S(1)}, f32[2,384]{1,0:T(2,128)S(1)}, u32[]{:S(2)}, u32[]{:S(2)}) %collective-permute-start.33) | collective-permute-done | bytes 3104 | tf_op jit(solution)/shard_map/ppermute | solution.py:479
  100.6 0.9 proj_add_sum.1
  (104 shorter events, 20.1 us)
Async XLA Ops:
  0.7 7.7 %collective-permute-start = (bf16[256,384]{1,0:T(8,128)(2,1)}, bf16[256,384]{1,0:T(8,128)(2,1)S(1)}, u32[]{:S(2)}, u32[]{:S(2)}) collective-permute-start(bf16[256,384]{1,0:T(8,128)(2,1)} %refs_1_.6), channel_id=1, source_target_pairs={{0,1},{1,0},{2,3},{3,2},{4,5},{5,4},{6,7},{7,6},{8,9},{9,8},{10,11... | collective-permute-start | bytes 589832 | tf_op jit(solution)/shard_map/ppermute | solution.py:479
  1.2 8.1 %collective-permute-start.1 = (bf16[256,384]{1,0:T(8,128)(2,1)}, bf16[256,384]{1,0:T(8,128)(2,1)S(1)}, u32[]{:S(2)}, u32[]{:S(2)}) collective-permute-start(bf16[256,384]{1,0:T(8,128)(2,1)} %refs_1_.7), channel_id=1, source_target_pairs={{0,1},{1,0},{2,3},{3,2},{4,5},{5,4},{6,7},{7,6},{8,9},{9,8},{10,11... | collective-permute-start | bytes 589832 | tf_op jit(solution)/shard_map/ppermute | solution.py:479
  1.3 8.9 %collective-permute-start.3 = (bf16[384,384]{1,0:T(8,128)(2,1)}, bf16[384,384]{1,0:T(8,128)(2,1)S(1)}, u32[]{:S(2)}, u32[]{:S(2)}) collective-permute-start(bf16[384,384]{1,0:T(8,128)(2,1)} %bitcast.33), channel_id=1, source_target_pairs={{0,1},{1,0},{2,3},{3,2},{4,5},{5,4},{6,7},{7,6},{8,9},{9,8},{10,11... | collective-permute-start | bytes 884744 | tf_op jit(solution)/shard_map/ppermute | solution.py:479
  1.7 8.5 %collective-permute-start.2 = (bf16[1152,384]{1,0:T(8,128)(2,1)}, bf16[1152,384]{1,0:T(8,128)(2,1)S(1)}, u32[]{:S(2)}, u32[]{:S(2)}) collective-permute-start(bf16[1152,384]{1,0:T(8,128)(2,1)} %bitcast.30), channel_id=1, source_target_pairs={{0,1},{1,0},{2,3},{3,2},{4,5},{5,4},{6,7},{7,6},{8,9},{9,8},{10,11... | collective-permute-start | bytes 2654216 | tf_op jit(solution)/shard_map/ppermute | solution.py:479
  5.4 4.8 %collective-permute-start.4 = (f32[16,384]{1,0:T(8,128)S(1)}, f32[16,384]{1,0:T(8,128)S(1)}, u32[]{:S(2)}, u32[]{:S(2)}) collective-permute-start(f32[16,384]{1,0:T(8,128)S(1)} %get-tuple-element.94.refs_0_.refs_3_), channel_id=1, source_target_pairs={{0,2},{2,0},{1,3},{3,1},{4,6},{6,4},{5,7},{7,5},{8,10},{10,8},{9,1... | collective-permute-start | bytes 73736 | tf_op jit(solution)/shard_map/ppermute | solution.py:475
  8.5 5.0 %collective-permute-start.5 = (bf16[512,384]{1,0:T(8,128)(2,1)S(1)}, bf16[512,384]{1,0:T(8,128)(2,1)S(1)}, u32[]{:S(2)}, u32[]{:S(2)}) collective-permute-start(bf16[512,384]{1,0:T(8,128)(2,1)S(1)} %pack.2.refs_0_), channel_id=1, source_target_pairs={{1,2},{2,1},{5,6},{6,5},{9,10},{10,9},{13,14},{14,13},{17,18},{18,... | collective-permute-start | bytes 1179656 | tf_op jit(solution)/shard_map/ppermute | solution.py:570
  12.2 12.6 %collective-permute-start.10 = (bf16[1536,384]{1,0:T(8,128)(2,1)S(1)}, bf16[1536,384]{1,0:T(8,128)(2,1)S(1)}, u32[]{:S(2)}, u32[]{:S(2)}) collective-permute-start(bf16[1536,384]{1,0:T(8,128)(2,1)S(1)} %copy-done.7), channel_id=1, source_target_pairs={{0,1},{1,0},{2,3},{3,2},{4,5},{5,4},{6,7},{7,6},{8,9},{9,8},{10,11... | collective-permute-start | bytes 3538952 | tf_op jit(solution)/shard_map/ppermute | solution.py:479
  12.5 21.4 %collective-permute-start.13 = (bf16[384,1536]{1,0:T(8,128)(2,1)S(1)}, bf16[384,1536]{1,0:T(8,128)(2,1)S(1)}, u32[]{:S(2)}, u32[]{:S(2)}) collective-permute-start(bf16[384,1536]{1,0:T(8,128)(2,1)S(1)} %copy-done.6), channel_id=1, source_target_pairs={{0,1},{1,0},{2,3},{3,2},{4,5},{5,4},{6,7},{7,6},{8,9},{9,8},{10,11... | collective-permute-start | bytes 3538952 | tf_op jit(solution)/shard_map/ppermute | solution.py:479
  12.8 11.5 %collective-permute-start.9 = (bf16[512,384]{1,0:T(8,128)(2,1)S(1)}, bf16[512,384]{1,0:T(8,128)(2,1)S(1)}, u32[]{:S(2)}, u32[]{:S(2)}) collective-permute-start(bf16[512,384]{1,0:T(8,128)(2,1)S(1)} %pack.3.refs_0_), channel_id=1, source_target_pairs={{1,2},{2,1},{5,6},{6,5},{9,10},{10,9},{13,14},{14,13},{17,18},{18,... | collective-permute-start | bytes 1179656 | tf_op jit(solution)/shard_map/ppermute | solution.py:572
  19.5 14.5 %collective-permute-start.12 = (bf16[256,768]{1,0:T(8,128)(2,1)S(1)}, bf16[256,768]{1,0:T(8,128)(2,1)S(1)}, u32[]{:S(2)}, u32[]{:S(2)}) collective-permute-start(bf16[256,768]{1,0:T(8,128)(2,1)S(1)} %get-tuple-element.100.refs_0_.refs_6_.refs_4_), channel_id=1, source_target_pairs={{0,2},{2,0},{1,3},{3,1},{4,6},{6,4},{5,7},{7,5},{8,10},{10,8},{9,1... | collective-permute-start | bytes 1179656 | tf_op jit(solution)/shard_map/ppermute | solution.py:475
  25.8 8.1 %collective-permute-start.11 = (bf16[256,384]{1,0:T(8,128)(2,1)S(1)}, bf16[256,384]{1,0:T(8,128)(2,1)S(1)}, u32[]{:S(2)}, u32[]{:S(2)}) collective-permute-start(bf16[256,384]{1,0:T(8,128)(2,1)S(1)} %get-tuple-element.103), channel_id=1, source_target_pairs={{0,1},{1,0},{2,3},{3,2},{4,5},{5,4},{6,7},{7,6},{8,9},{9,8},{10,11... | collective-permute-start | bytes 589832 | tf_op jit(solution)/shard_map/ppermute | solution.py:479
  36.9 6.1 %collective-permute-start.15 = (bf16[256,1920]{1,0:T(8,128)(2,1)S(1)}, bf16[256,1920]{1,0:T(8,128)(2,1)S(1)}, u32[]{:S(2)}, u32[]{:S(2)}) collective-permute-start(bf16[256,1920]{1,0:T(8,128)(2,1)S(1)} %get-tuple-element.114.refs_2_), channel_id=1, source_target_pairs={{0,1},{1,0},{2,3},{3,2},{4,5},{5,4},{6,7},{7,6},{8,9},{9,8},{10,11... | collective-permute-start | bytes 2949128 | tf_op jit(solution)/shard_map/ppermute | solution.py:479
  37.1 3.6 %collective-permute-start.14 = (bf16[256,1536]{1,0:T(8,128)(2,1)S(1)}, bf16[256,1536]{1,0:T(8,128)(2,1)S(1)}, u32[]{:S(2)}, u32[]{:S(2)}) collective-permute-start(bf16[256,1536]{1,0:T(8,128)(2,1)S(1)} %get-tuple-element.108.active.refs_3_), channel_id=1, source_target_pairs={{0,1},{1,0},{2,3},{3,2},{4,5},{5,4},{6,7},{7,6},{8,9},{9,8},{10,11... | collective-permute-start | bytes 2359304 | tf_op jit(solution)/shard_map/ppermute | solution.py:479
  37.5 11.1 %collective-permute-start.16 = (bf16[256,768]{1,0:T(8,128)(2,1)S(1)}, bf16[256,768]{1,0:T(8,128)(2,1)S(1)}, u32[]{:S(2)}, u32[]{:S(2)}) collective-permute-start(bf16[256,768]{1,0:T(8,128)(2,1)S(1)} %get-tuple-element.119.refs_5_.refs_6_), channel_id=1, source_target_pairs={{0,2},{2,0},{1,3},{3,1},{4,6},{6,4},{5,7},{7,5},{8,10},{10,8},{9,1... | collective-permute-start | bytes 1179656 | tf_op jit(solution)/shard_map/ppermute | solution.py:475
  41.5 15.4 %collective-permute-start.17 = (bf16[4,48,1536]{2,1,0:T(8,128)(2,1)S(1)}, bf16[4,48,1536]{2,1,0:T(8,128)(2,1)S(1)}, u32[]{:S(2)}, u32[]{:S(2)}) collective-permute-start(bf16[4,48,1536]{2,1,0:T(8,128)(2,1)S(1)} %get-tuple-element.112.refs_0_), channel_id=1, source_target_pairs={{0,4},{4,0},{8,12},{12,8},{16,20},{20,16},{24,28},{28,24},{1,5},{5... | collective-permute-start | bytes 1769480 | tf_op jit(solution)/shard_map/ppermute | solution.py:487
  44.3 15.2 %collective-permute-start.18 = (bf16[4,192,384]{2,1,0:T(8,128)(2,1)S(1)}, bf16[4,192,384]{2,1,0:T(8,128)(2,1)S(1)}, u32[]{:S(2)}, u32[]{:S(2)}) collective-permute-start(bf16[4,192,384]{2,1,0:T(8,128)(2,1)S(1)} %get-tuple-element.115.refs_0_), channel_id=1, source_target_pairs={{0,8},{4,12},{8,0},{12,4},{16,24},{20,28},{24,16},{28,20},{1,9},{5... | collective-permute-start | bytes 1769480 | tf_op jit(solution)/shard_map/ppermute | solution.py:487
  53.1 9.2 %collective-permute-start.19 = (bf16[1536,256]{1,0:T(8,128)(2,1)S(1)}, bf16[1536,256]{1,0:T(8,128)(2,1)S(1)}, u32[]{:S(2)}, u32[]{:S(2)}) collective-permute-start(bf16[1536,256]{1,0:T(8,128)(2,1)S(1)} %get-tuple-element.128.refs_3_), channel_id=1, source_target_pairs={{0,1},{1,0},{2,3},{3,2},{4,5},{5,4},{6,7},{7,6},{8,9},{9,8},{10,11... | collective-permute-start | bytes 2359304 | tf_op jit(solution)/shard_map/ppermute | solution.py:479
  53.1 12.1 %collective-permute-start.20 = (bf16[272,768]{1,0:T(8,128)(2,1)S(1)}, bf16[272,768]{1,0:T(8,128)(2,1)S(1)}, u32[]{:S(2)}, u32[]{:S(2)}) collective-permute-start(bf16[272,768]{1,0:T(8,128)(2,1)S(1)} %get-tuple-element.122.refs_0_.refs_10_), channel_id=1, source_target_pairs={{0,2},{2,0},{1,3},{3,1},{4,6},{6,4},{5,7},{7,5},{8,10},{10,8},{9,1... | collective-permute-start | bytes 1253384 | tf_op jit(solution)/shard_map/ppermute | solution.py:475
  54.1 18.3 %collective-permute-start.23 = (bf16[256,768]{1,0:T(8,128)(2,1)S(1)}, bf16[256,768]{1,0:T(8,128)(2,1)S(1)}, u32[]{:S(2)}, u32[]{:S(2)}) collective-permute-start(bf16[256,768]{1,0:T(8,128)(2,1)S(1)} %get-tuple-element.141.refs_0_.refs_6_), channel_id=1, source_target_pairs={{1,3},{2,0},{5,7},{6,4},{9,11},{10,8},{13,15},{14,12},{17,19},{18,... | collective-permute-start | bytes 1179656 | tf_op jit(solution)/shard_map/ppermute | solution.py:647
  57.1 15.1 %collective-permute-start.21 = (bf16[2,48,1536]{2,1,0:T(8,128)(2,1)S(1)}, bf16[2,48,1536]{2,1,0:T(8,128)(2,1)S(1)}, u32[]{:S(2)}, u32[]{:S(2)}) collective-permute-start(bf16[2,48,1536]{2,1,0:T(8,128)(2,1)S(1)} %get-tuple-element.133), channel_id=1, source_target_pairs={{0,8},{4,12},{8,0},{12,4},{16,24},{20,28},{24,16},{28,20},{1,9},{5... | collective-permute-start | bytes 884744 | tf_op jit(solution)/shard_map/ppermute | solution.py:487
  59.6 17.6 %collective-permute-start.27 = (bf16[2,192,384]{2,1,0:T(8,128)(2,1)S(1)}, bf16[2,192,384]{2,1,0:T(8,128)(2,1)S(1)}, u32[]{:S(2)}, u32[]{:S(2)}) collective-permute-start(bf16[2,192,384]{2,1,0:T(8,128)(2,1)S(1)} %get-tuple-element.148), channel_id=1, source_target_pairs={{0,16},{4,20},{8,24},{12,28},{16,0},{20,4},{24,8},{28,12},{1,17},{... | collective-permute-start | bytes 884744 | tf_op jit(solution)/shard_map/ppermute | solution.py:487
  63.7 14.2 %collective-permute-start.28 = (bf16[4,48,1536]{2,1,0:T(8,128)(2,1)S(1)}, bf16[4,48,1536]{2,1,0:T(8,128)(2,1)S(1)}, u32[]{:S(2)}, u32[]{:S(2)}) collective-permute-start(bf16[4,48,1536]{2,1,0:T(8,128)(2,1)S(1)} %get-tuple-element.130.refs_0_), channel_id=1, source_target_pairs={{0,4},{4,0},{8,12},{12,8},{16,20},{20,16},{24,28},{28,24},{1,5},{5... | collective-permute-start | bytes 1769480 | tf_op jit(solution)/shard_map/ppermute | solution.py:487
  66.4 5.8 %collective-permute-start.22 = (f32[6,384]{1,0:T(8,128)S(1)}, f32[6,384]{1,0:T(8,128)S(1)}, u32[]{:S(2)}, u32[]{:S(2)}) collective-permute-start(f32[6,384]{1,0:T(8,128)S(1)} %get-tuple-element.135), channel_id=1, source_target_pairs={{0,1},{1,0},{2,3},{3,2},{4,5},{5,4},{6,7},{7,6},{8,9},{9,8},{10,11... | collective-permute-start | bytes 27656 | tf_op jit(solution)/shard_map/ppermute | solution.py:479
  72.3 4.9 %collective-permute-start.26 = (f32[1,24,384]{2,1,0:T(8,128)S(1)}, f32[1,24,384]{2,1,0:T(8,128)S(1)}, u32[]{:S(2)}, u32[]{:S(2)}) collective-permute-start(f32[1,24,384]{2,1,0:T(8,128)S(1)} %payload.1.refs_0_.refs_1_), channel_id=1, source_target_pairs={{0,16},{4,20},{8,24},{12,28},{16,0},{20,4},{24,8},{28,12},{1,17},{... | collective-permute-start | bytes 110600 | tf_op jit(solution)/shard_map/ppermute | solution.py:487
  78.0 11.0 %collective-permute-start.29 = (bf16[2,48,1536]{2,1,0:T(8,128)(2,1)S(1)}, bf16[2,48,1536]{2,1,0:T(8,128)(2,1)S(1)}, u32[]{:S(2)}, u32[]{:S(2)}) collective-permute-start(bf16[2,48,1536]{2,1,0:T(8,128)(2,1)S(1)} %get-tuple-element.152), channel_id=1, source_target_pairs={{0,8},{4,12},{8,0},{12,4},{16,24},{20,28},{24,16},{28,20},{1,9},{5... | collective-permute-start | bytes 884744 | tf_op jit(solution)/shard_map/ppermute | solution.py:487
  79.5 18.3 %collective-permute-start.25 = (f32[256,384]{1,0:T(8,128)S(1)}, f32[256,384]{1,0:T(8,128)S(1)}, u32[]{:S(2)}, u32[]{:S(2)}) collective-permute-start(f32[256,384]{1,0:T(8,128)S(1)} %get-tuple-element.146), channel_id=1, source_target_pairs={{0,1},{1,0},{2,3},{3,2},{4,5},{5,4},{6,7},{7,6},{8,9},{9,8},{10,11... | collective-permute-start | bytes 1179656 | tf_op jit(solution)/shard_map/ppermute | solution.py:479
  79.5 10.3 %collective-permute-start.30 = (f32[2,24,384]{2,1,0:T(8,128)S(1)}, f32[2,24,384]{2,1,0:T(8,128)S(1)}, u32[]{:S(2)}, u32[]{:S(2)}) collective-permute-start(f32[2,24,384]{2,1,0:T(8,128)S(1)} %join.3.refs_0_.refs_1_), channel_id=1, source_target_pairs={{0,8},{4,12},{8,0},{12,4},{16,24},{20,28},{24,16},{28,20},{1,9},{5... | collective-permute-start | bytes 221192 | tf_op jit(solution)/shard_map/ppermute | solution.py:487
  80.1 11.9 %collective-permute-start.31 = (bf16[1,48,1536]{2,1,0:T(8,128)(2,1)S(1)}, bf16[1,48,1536]{2,1,0:T(8,128)(2,1)S(1)}, u32[]{:S(2)}, u32[]{:S(2)}) collective-permute-start(bf16[1,48,1536]{2,1,0:T(8,128)(2,1)S(1)} %get-tuple-element.154), channel_id=1, source_target_pairs={{0,16},{4,20},{8,24},{12,28},{16,0},{20,4},{24,8},{28,12},{1,17},{... | collective-permute-start | bytes 442376 | tf_op jit(solution)/shard_map/ppermute | solution.py:487
  81.1 16.7 %collective-permute-start.24 = (bf16[256,384]{1,0:T(8,128)(2,1)S(1)}, bf16[256,384]{1,0:T(8,128)(2,1)S(1)}, u32[]{:S(2)}, u32[]{:S(2)}) collective-permute-start(bf16[256,384]{1,0:T(8,128)(2,1)S(1)} %get-tuple-element.143), channel_id=1, source_target_pairs={{0,1},{1,0},{2,3},{3,2},{4,5},{5,4},{6,7},{7,6},{8,9},{9,8},{10,11... | collective-permute-start | bytes 589832 | tf_op jit(solution)/shard_map/ppermute | solution.py:479
  89.8 5.3 %collective-permute-start.32 = (f32[4,24,384]{2,1,0:T(8,128)S(1)}, f32[4,24,384]{2,1,0:T(8,128)S(1)}, u32[]{:S(2)}, u32[]{:S(2)}) collective-permute-start(f32[4,24,384]{2,1,0:T(8,128)S(1)} %join.4.refs_0_.refs_1_), channel_id=1, source_target_pairs={{0,4},{4,0},{8,12},{12,8},{16,20},{20,16},{24,28},{28,24},{1,5},{5... | collective-permute-start | bytes 442376 | tf_op jit(solution)/shard_map/ppermute | solution.py:487
  92.0 7.9 %collective-permute-start.34 = (bf16[1,192,384]{2,1,0:T(8,128)(2,1)S(1)}, bf16[1,192,384]{2,1,0:T(8,128)(2,1)S(1)}, u32[]{:S(2)}, u32[]{:S(2)}) collective-permute-start(bf16[1,192,384]{2,1,0:T(8,128)(2,1)S(1)} %get-tuple-element.164), channel_id=1, source_target_pairs={{0,4},{4,0},{8,12},{12,8},{16,20},{20,16},{24,28},{28,24},{1,5},{5... | collective-permute-start | bytes 442376 | tf_op jit(solution)/shard_map/ppermute | solution.py:487
  92.1 8.6 %collective-permute-start.35 = (bf16[1,48,1536]{2,1,0:T(8,128)(2,1)S(1)}, bf16[1,48,1536]{2,1,0:T(8,128)(2,1)S(1)}, u32[]{:S(2)}, u32[]{:S(2)}) collective-permute-start(bf16[1,48,1536]{2,1,0:T(8,128)(2,1)S(1)} %get-tuple-element.166), channel_id=1, source_target_pairs={{0,16},{4,20},{8,24},{12,28},{16,0},{20,4},{24,8},{28,12},{1,17},{... | collective-permute-start | bytes 442376 | tf_op jit(solution)/shard_map/ppermute | solution.py:487
  (18 other events, 51.3 us)
